TPU v7x, 32 devices: a whole 2x2x4 slice. The times are simulated.
32 devices in a mesh: dp: 8 (over z, y), mp: 4 (over x, core).
Axes of the slice: x: 2, y: 2, z: 4, core: 2. Of those that a mesh axis runs over, the one named last changes fastest.
Arguments:
- hidden_rows: bfloat16 [16384, 768], P(('dp', 'mp')), may hold values from -6 to 6
- token_table: bfloat16 [4096, 768], replicated, may hold values from -6 to 6
- masked_positions: int32 [128, 32], P(('dp', 'mp')), may hold values from 0 to 127, as said below
- masked_counts: int32 [128], P(('dp', 'mp')), may hold values from 6 to 32, as said below
- replace_rows: int32 [128, 32], P(('dp', 'mp')), may hold values from 0 to 4095
- masked_cotangent: bfloat16 [128, 32, 768], P(('dp', 'mp')), may hold values from -6 to 6
- step_number: int32 [1], replicated, may hold values from 2 to 20
- attend_master: float32 [768, 2304], P('dp', 'mp'), may hold values from -0.21875 to 0.21875
- merge_master: float32 [768, 768], P('dp', 'mp'), may hold values from -0.625 to 0.625
- norms_master: float32 [4, 768], P('mp', 'dp'), may hold values from 0.5 to 1.5
- gate_master: float32 [768, 3072], P('dp', 'mp'), may hold values from -0.21875 to 0.21875
- value_master: float32 [768, 3072], P('dp', 'mp'), may hold values from -0.21875 to 0.21875
- down_master: float32 [3072, 768], P('mp', 'dp'), may hold values from -0.109375 to 0.109375
- first_attend: float32 [768, 2304], P('dp', 'mp'), may hold values from -24 to 24
- first_merge: float32 [768, 768], P('dp', 'mp'), may hold values from -14 to 14
- first_norms: float32 [4, 768], P('mp', 'dp'), may hold values from -32 to 32
- first_gate: float32 [768, 3072], P('dp', 'mp'), may hold values from -20 to 20
- first_value: float32 [768, 3072], P('dp', 'mp'), may hold values from -14 to 14
- first_down: float32 [3072, 768], P('mp', 'dp'), may hold values from -28 to 28
- second_attend: float32 [768, 2304], P('dp', 'mp'), may hold values from 1.032192 to 8.84736
- second_merge: float32 [768, 768], P('dp', 'mp'), may hold values from 0.262144 to 2.21184
- second_norms: float32 [4, 768], P('mp', 'dp'), may hold values from 1.572864 to 13.43488
- second_gate: float32 [768, 3072], P('dp', 'mp'), may hold values from 0.606208 to 5.24288
- second_value: float32 [768, 3072], P('dp', 'mp'), may hold values from 0.278528 to 2.359296
- second_down: float32 [3072, 768], P('mp', 'dp'), may hold values from 1.097728 to 9.50272
Outputs:
- layer_output: bfloat16 [16384, 768], P(('dp', 'mp'))
- input_gradient: float32 [16384, 768], P(('dp', 'mp'))
- gradient_attend: float32 [768, 2304], P('dp', 'mp')
- gradient_merge: float32 [768, 768], P('dp', 'mp')
- gradient_norms: float32 [4, 768], P('mp', 'dp')
- gradient_gate: float32 [768, 3072], P('dp', 'mp')
- gradient_value: float32 [768, 3072], P('dp', 'mp')
- gradient_down: float32 [3072, 768], P('mp', 'dp')
- moment_attend: float32 [768, 2304], P('dp', 'mp')
- moment_merge: float32 [768, 768], P('dp', 'mp')
- moment_norms: float32 [4, 768], P('mp', 'dp')
- moment_gate: float32 [768, 3072], P('dp', 'mp')
- moment_value: float32 [768, 3072], P('dp', 'mp')
- moment_down: float32 [3072, 768], P('mp', 'dp')
- squares_attend: float32 [768, 2304], P('dp', 'mp')
- squares_merge: float32 [768, 768], P('dp', 'mp')
- squares_norms: float32 [4, 768], P('mp', 'dp')
- squares_gate: float32 [768, 3072], P('dp', 'mp')
- squares_value: float32 [768, 3072], P('dp', 'mp')
- squares_down: float32 [3072, 768], P('mp', 'dp')
- updated_attend: float32 [768, 2304], P('dp', 'mp')
- updated_merge: float32 [768, 768], P('dp', 'mp')
- updated_norms: float32 [4, 768], P('mp', 'dp')
- updated_gate: float32 [768, 3072], P('dp', 'mp')
- updated_value: float32 [768, 3072], P('dp', 'mp')
- updated_down: float32 [3072, 768], P('mp', 'dp')
Inputs may be any that keep to these rules, and one draw needn't show every extreme that they name: `masked_positions`: each row holds 32 different positions. Slots masked_counts[n] and later of sequence n are not live and are ignored, together with their replace_rows and masked_cotangent entries. Some sequence has exactly 32 live slots and some exactly the least value.
All inputs are finite; a program needn't handle non-finite values.
Results may differ from a plain program's by a relative error of at most 0.013.
The roundings to bfloat16 on the way count: a program that leaves them out, or rounds other values in their place, can miss the bound.
Values may be sent and summed in bfloat16 or wider, within the bound.
No kernel may reach another device: no remote copies, remote signals or barrier semaphores. Data moves between devices by JAX's collectives and lax.ppermute only.
A program may use at most 192 MiB of HBM per device.

v0:
```python
from functools import partial

import jax
import jax.numpy as jnp
from jax import lax
from jax.sharding import PartitionSpec as P

HEADS = 12
HEAD_DIM = 64


beta_one = 0.9
beta_two = 0.999
peak_rate = 1.0
warm_steps = 4.0
total_steps = 100.0
decay_rate = 0.01
adam_eps = 1e-08
norm_eps = 1e-05


def layer_norm(row_data, gain_row, shift_row):
    centered = row_data - jnp.mean(row_data, axis=-1, keepdims=True)
    spread = jnp.mean(centered * centered, axis=-1, keepdims=True)
    return centered * lax.rsqrt(spread + norm_eps) * gain_row + shift_row


def alibi_table(head_count, seq_len):
    slopes = jnp.exp2(-8.0 * jnp.arange(1, head_count + 1, dtype=jnp.float32) / head_count)
    places = jnp.arange(seq_len, dtype=jnp.float32)
    return slopes[:, None, None] * jnp.abs(places[:, None] - places[None, :])


def right_transposed(left_op, right_op):
    return lax.dot_general(
        left_op, right_op, (((1,), (1,)), ((), ())), preferred_element_type=jnp.float32
    )


def left_transposed(left_op, right_op):
    return lax.dot_general(
        left_op, right_op, (((0,), (0,)), ((), ())), preferred_element_type=jnp.float32
    )


def geglu_rows(gate_in, value_in):
    return jax.nn.gelu(gate_in, approximate=False) * value_in


def ffn_front(ffn_rows, gate_full, value_full):
    gated = jnp.dot(ffn_rows, gate_full, preferred_element_type=jnp.float32)
    valued = jnp.dot(ffn_rows, value_full, preferred_element_type=jnp.float32)
    return (gated, valued, geglu_rows(gated, valued).astype(jnp.bfloat16))


def ffn_grads(ffn_rows, gated, valued, hidden, pulled, down_full):
    hidden_back = right_transposed(pulled, down_full)
    _, pullback = jax.vjp(geglu_rows, gated, valued)
    gate_back, value_back = pullback(hidden_back)
    gate_back = gate_back.astype(jnp.bfloat16)
    value_back = value_back.astype(jnp.bfloat16)
    return (
        gate_back,
        value_back,
        left_transposed(ffn_rows, gate_back),
        left_transposed(ffn_rows, value_back),
        left_transposed(hidden, pulled),
    )


def attend_block(block_mix, alibi):
    seq_count, length = (block_mix.shape[0], block_mix.shape[1])
    queries = block_mix[:, :, 0]
    key_rows = block_mix[:, :, 1]
    value_rows = block_mix[:, :, 2]
    scores = (
        jnp.einsum("bshe,bthe->bhst", queries, key_rows, preferred_element_type=jnp.float32)
        * HEAD_DIM ** (-0.5)
        - alibi
    )
    row_max = jnp.max(scores, axis=-1, keepdims=True)
    exp_scores = jnp.exp(scores - row_max)
    row_total = jnp.sum(exp_scores, axis=-1, keepdims=True)
    probs = (exp_scores / row_total).astype(jnp.bfloat16)
    attended = jnp.einsum("bhst,bthe->bshe", probs, value_rows, preferred_element_type=jnp.float32)
    return (
        attended.reshape(seq_count, length, -1).astype(jnp.bfloat16),
        row_max + jnp.log(row_total),
    )


def attend_back(block_mix, log_total, attended_back, alibi):
    seq_count, length = (block_mix.shape[0], block_mix.shape[1])
    scale = HEAD_DIM ** (-0.5)
    queries = block_mix[:, :, 0]
    key_rows = block_mix[:, :, 1]
    value_rows = block_mix[:, :, 2]
    scores = (
        jnp.einsum("bshe,bthe->bhst", queries, key_rows, preferred_element_type=jnp.float32) * scale
        - alibi
    )
    probs = jnp.exp(scores - log_total)
    heads_back = attended_back.reshape(queries.shape)
    probs_back = jnp.einsum(
        "bshe,bthe->bhst", heads_back, value_rows, preferred_element_type=jnp.float32
    )
    inner = jnp.sum(probs * probs_back, axis=-1, keepdims=True)
    scores_back = (probs * (probs_back - inner)).astype(jnp.bfloat16)
    queries_back = (
        jnp.einsum("bhst,bthe->bshe", scores_back, key_rows, preferred_element_type=jnp.float32)
        * scale
    )
    keys_back = (
        jnp.einsum("bhst,bshe->bthe", scores_back, queries, preferred_element_type=jnp.float32)
        * scale
    )
    values_back = jnp.einsum(
        "bhst,bshe->bthe",
        probs.astype(jnp.bfloat16),
        heads_back,
        preferred_element_type=jnp.float32,
    )
    stacked = jnp.stack([queries_back, keys_back, values_back], axis=2).astype(jnp.bfloat16)
    return stacked.reshape(seq_count, length, -1)


def adamw_step(master, first, second, gradient, step_value, decay):
    step_rate = peak_rate * jnp.minimum(
        step_value / warm_steps, (total_steps - step_value) / (total_steps - warm_steps)
    )
    fix_one = 1.0 - jnp.power(jnp.float32(beta_one), step_value)
    fix_two = 1.0 - jnp.power(jnp.float32(beta_two), step_value)
    moment = beta_one * first + (1.0 - beta_one) * gradient
    squares = beta_two * second + (1.0 - beta_two) * gradient * gradient
    updated = master - step_rate * (
        moment / fix_one / (jnp.sqrt(squares / fix_two) + adam_eps) + decay * master
    )
    return (moment, squares, updated)


def shards(
    hidden_rows,
    token_table,
    masked_positions,
    masked_counts,
    replace_rows,
    masked_cotangent,
    step_number,
    attend_master,
    merge_master,
    norms_master,
    gate_master,
    value_master,
    down_master,
    first_attend,
    first_merge,
    first_norms,
    first_gate,
    first_value,
    first_down,
    second_attend,
    second_merge,
    second_norms,
    second_gate,
    second_value,
    second_down,
):
    local_seqs, slot_count = masked_positions.shape
    local_rows, model_width = hidden_rows.shape
    length = local_rows // local_seqs
    dp_size = lax.axis_size("dp")
    mp_size = lax.axis_size("mp")
    live_slots = jnp.arange(slot_count, dtype=jnp.int32)[None, :] < masked_counts[:, None]
    place_bool = (
        masked_positions[:, :, None] == jnp.arange(length, dtype=jnp.int32)[None, None, :]
    ) & live_slots[:, :, None]
    place_low = place_bool.astype(jnp.bfloat16)
    chosen = jnp.take(token_table, replace_rows.reshape(-1), axis=0).reshape(
        local_seqs, slot_count, model_width
    )
    swapped = jnp.einsum(
        "sjt,sjd->std", place_low, chosen, preferred_element_type=jnp.float32
    ).astype(jnp.bfloat16)
    replaced = jnp.any(place_bool, axis=1)[:, :, None]
    start_rows = jnp.where(
        replaced, swapped, hidden_rows.reshape(local_seqs, length, model_width)
    ).reshape(local_rows, model_width)
    cotangent_rows = jnp.einsum(
        "sjt,sjd->std", place_low, masked_cotangent, preferred_element_type=jnp.float32
    ).reshape(local_rows, model_width)
    attend_rows, merge_rows, gate_rows, value_rows, down_cols = (
        lax.all_gather(attend_master.astype(jnp.bfloat16), "dp", axis=0, tiled=True),
        lax.all_gather(merge_master.astype(jnp.bfloat16), "dp", axis=0, tiled=True),
        lax.all_gather(gate_master.astype(jnp.bfloat16), "dp", axis=0, tiled=True),
        lax.all_gather(value_master.astype(jnp.bfloat16), "dp", axis=0, tiled=True),
        lax.all_gather(down_master.astype(jnp.bfloat16), "dp", axis=1, tiled=True),
    )
    norm_rows = norms_master.shape[0]
    norm_piece = lax.all_gather(norms_master, ("dp", "mp"), axis=1, tiled=True)
    norms = (
        norm_piece.reshape(norm_rows, dp_size, mp_size, -1)
        .transpose(2, 0, 1, 3)
        .reshape(norm_rows * mp_size, -1)
    )
    attend_full, merge_full = (
        lax.all_gather(attend_rows, "mp", axis=1, tiled=True),
        lax.all_gather(merge_rows, "mp", axis=1, tiled=True),
    )
    gate_full, value_full, down_full = (gate_rows, value_rows, down_cols)
    alibi = alibi_table(HEADS, length)
    block_seqs = min(4, local_seqs)
    mixed = jnp.dot(start_rows, attend_full, preferred_element_type=jnp.float32).astype(
        jnp.bfloat16
    )
    mixed_blocks = mixed.reshape(local_seqs // block_seqs, block_seqs, length, 3, HEADS, HEAD_DIM)
    attended, log_totals = lax.map(partial(attend_block, alibi=alibi), mixed_blocks)
    attended_rows = attended.reshape(local_rows, model_width)
    first_sum = start_rows.astype(jnp.float32) + jnp.dot(
        attended_rows, merge_full, preferred_element_type=jnp.float32
    )
    normed = layer_norm(first_sum, norms[0], norms[1])
    narrow = normed.astype(jnp.bfloat16)
    ffn_rows = lax.all_gather(narrow, "mp", axis=0, tiled=True)
    gated, valued, hidden = ffn_front(ffn_rows, gate_full, value_full)
    ffn_out = lax.psum_scatter(
        jnp.dot(hidden, down_full, preferred_element_type=jnp.float32),
        "mp",
        scatter_dimension=0,
        tiled=True,
    )
    second_sum = normed + ffn_out
    layer_output = layer_norm(second_sum, norms[2], norms[3]).astype(jnp.bfloat16)
    _, second_pull = jax.vjp(layer_norm, second_sum, norms[2], norms[3])
    second_back, gain_two_back, shift_two_back = second_pull(cotangent_rows)
    pulled = second_back.astype(jnp.bfloat16)
    work_pull = lax.all_gather(pulled, "mp", axis=0, tiled=True)
    work_gated, work_valued, work_hidden = (gated, valued, hidden)
    gate_back, value_back, gate_grad, value_grad, down_grad = ffn_grads(
        ffn_rows, work_gated, work_valued, work_hidden, work_pull, down_full
    )
    gate_part = gate_back
    value_part = value_back
    normed_back = lax.psum_scatter(
        right_transposed(gate_part, gate_full) + right_transposed(value_part, value_full),
        "mp",
        scatter_dimension=0,
        tiled=True,
    )
    _, first_pull = jax.vjp(layer_norm, first_sum, norms[0], norms[1])
    first_back, gain_one_back, shift_one_back = first_pull(normed_back + second_back)
    branch_pull = first_back.astype(jnp.bfloat16)
    merge_grad = left_transposed(attended_rows, branch_pull)
    attended_back = right_transposed(branch_pull, merge_full).astype(jnp.bfloat16)
    mixed_back = lax.map(
        lambda pieces: attend_back(pieces[0], pieces[1], pieces[2], alibi),
        (mixed_blocks, log_totals, attended_back.reshape(attended.shape)),
    )
    mixed_back = mixed_back.reshape(local_rows, 3 * model_width)
    attend_grad = left_transposed(start_rows, mixed_back)
    input_gradient = first_back + right_transposed(mixed_back, attend_full)
    attend_part, merge_part = (
        lax.psum_scatter(attend_grad, "mp", scatter_dimension=1, tiled=True),
        lax.psum_scatter(merge_grad, "mp", scatter_dimension=1, tiled=True),
    )
    gate_part, value_part, down_part = (gate_grad, value_grad, down_grad)
    gradient_attend, gradient_merge, gradient_gate, gradient_value, gradient_down = (
        lax.psum_scatter(attend_part, "dp", scatter_dimension=0, tiled=True),
        lax.psum_scatter(merge_part, "dp", scatter_dimension=0, tiled=True),
        lax.psum_scatter(gate_part, "dp", scatter_dimension=0, tiled=True),
        lax.psum_scatter(value_part, "dp", scatter_dimension=0, tiled=True),
        lax.psum_scatter(down_part, "dp", scatter_dimension=1, tiled=True),
    )
    norm_full = jnp.stack([gain_one_back, shift_one_back, gain_two_back, shift_two_back], axis=0)
    norm_sent = (
        norm_full.reshape(mp_size, norm_rows, dp_size, -1)
        .transpose(1, 2, 0, 3)
        .reshape(norm_rows, -1)
    )
    gradient_norms = lax.psum_scatter(norm_sent, ("dp", "mp"), scatter_dimension=1, tiled=True)
    step_value = step_number[0].astype(jnp.float32)
    moment_attend, squares_attend, updated_attend = adamw_step(
        attend_master, first_attend, second_attend, gradient_attend, step_value, decay_rate
    )
    moment_merge, squares_merge, updated_merge = adamw_step(
        merge_master, first_merge, second_merge, gradient_merge, step_value, decay_rate
    )
    moment_norms, squares_norms, updated_norms = adamw_step(
        norms_master, first_norms, second_norms, gradient_norms, step_value, 0.0
    )
    moment_gate, squares_gate, updated_gate = adamw_step(
        gate_master, first_gate, second_gate, gradient_gate, step_value, decay_rate
    )
    moment_value, squares_value, updated_value = adamw_step(
        value_master, first_value, second_value, gradient_value, step_value, decay_rate
    )
    moment_down, squares_down, updated_down = adamw_step(
        down_master, first_down, second_down, gradient_down, step_value, decay_rate
    )
    return (
        layer_output,
        input_gradient,
        gradient_attend,
        gradient_merge,
        gradient_norms,
        gradient_gate,
        gradient_value,
        gradient_down,
        moment_attend,
        moment_merge,
        moment_norms,
        moment_gate,
        moment_value,
        moment_down,
        squares_attend,
        squares_merge,
        squares_norms,
        squares_gate,
        squares_value,
        squares_down,
        updated_attend,
        updated_merge,
        updated_norms,
        updated_gate,
        updated_value,
        updated_down,
    )


def solution(mesh):
    return jax.shard_map(
        shards,
        mesh=mesh,
        in_specs=(
            P(("dp", "mp"), None),
            P(),
            P(("dp", "mp"), None),
            P(("dp", "mp")),
            P(("dp", "mp"), None),
            P(("dp", "mp"), None, None),
            P(),
            P("dp", "mp"),
            P("dp", "mp"),
            P("mp", "dp"),
            P("dp", "mp"),
            P("dp", "mp"),
            P("mp", "dp"),
            P("dp", "mp"),
            P("dp", "mp"),
            P("mp", "dp"),
            P("dp", "mp"),
            P("dp", "mp"),
            P("mp", "dp"),
            P("dp", "mp"),
            P("dp", "mp"),
            P("mp", "dp"),
            P("dp", "mp"),
            P("dp", "mp"),
            P("mp", "dp"),
        ),
        out_specs=(
            P(("dp", "mp"), None),
            P(("dp", "mp"), None),
            P("dp", "mp"),
            P("dp", "mp"),
            P("mp", "dp"),
            P("dp", "mp"),
            P("dp", "mp"),
            P("mp", "dp"),
            P("dp", "mp"),
            P("dp", "mp"),
            P("mp", "dp"),
            P("dp", "mp"),
            P("dp", "mp"),
            P("mp", "dp"),
            P("dp", "mp"),
            P("dp", "mp"),
            P("mp", "dp"),
            P("dp", "mp"),
            P("dp", "mp"),
            P("mp", "dp"),
            P("dp", "mp"),
            P("dp", "mp"),
            P("mp", "dp"),
            P("dp", "mp"),
            P("dp", "mp"),
            P("mp", "dp"),
        ),
        check_vma=False,
    )
```

profile of v0, /device:TPU:0, one launch (start us, length us, event | category | flops | bytes accessed | tf_op | source)
XLA Modules:
  0.0 1008.7 jit_solution(3584575890233740780)
XLA Ops:
  7.3 1.1 convert_element_type.93
  8.4 34.4 %all_gather.30 = bf16[768,576]{1,0:T(8,128)(2,1)S(1)} all-gather(bf16[96,576]{1,0:T(8,128)(2,1)S(1)} %convert_element_type.93), channel_id=1, replica_groups=mesh['dp'=8,'mp'=4] {'dp'}, dimensions={0}, use_global_device_ids=true | all-gather | bytes 995328 | tf_op jit(solution)/shard_map/all_gather | solution.py:192
  42.8 1.3 copy.136
  44.2 31.1 %all_gather.32 = bf16[768,192]{1,0:T(8,128)(2,1)S(1)} all-gather(bf16[96,192]{1,0:T(8,128)(2,1)S(1)} %convert_element_type.99), channel_id=1, replica_groups=mesh['dp'=8,'mp'=4] {'dp'}, dimensions={0}, use_global_device_ids=true | all-gather | bytes 331776 | tf_op jit(solution)/shard_map/all_gather | solution.py:193
  77.4 39.8 %all-reduce = f32[3072]{0:T(1024)S(1)} all-reduce(f32[3072]{0:T(1024)S(1)} %bitcast_dynamic-update-slice_fusion), channel_id=1, replica_groups=mesh['dp'=8,'mp'=4] {'dp','mp'}, use_global_device_ids=true, to_apply=%add | all-reduce | flops 3072 | bytes 24576
  117.5 1.0 broadcast_multiply_fusion
  118.6 4.6 gather_fusion
  123.8 4.3 convolution_convert_fusion
  128.1 2.5 copy.137
  130.6 4.2 squeeze.32
  134.8 1.0 fusion.70
  138.2 1.5 copy.142
  139.7 2.6 fusion.72
  143.5 1.2 fusion.28
  144.7 1.6 convert_element_type.102
  146.5 1.6 convert_element_type.104
  148.4 25.4 %all-gather.12.cloned.1.call-done = bf16[2048,768]{1,0:T(8,128)(2,1)} async-done(((bf16[512,768]{1,0:T(8,128)(2,1)}), bf16[2048,768]{1,0:T(8,128)(2,1)}) %all-gather.12.cloned.1.call-update) | async-done | bytes 3145744 | tf_op jit(solution)/shard_map/all_gather | solution.py:223
  173.8 7.5 fusion.74
  181.3 36.2 %all-gather.16.cloned.1.call-done = bf16[768,768]{1,0:T(8,128)(2,1)} async-done(((bf16[96,768]{1,0:T(8,128)(2,1)}), bf16[768,768]{1,0:T(8,128)(2,1)}) %all-gather.16.cloned.1.call-update) | async-done | bytes 1179664 | tf_op jit(solution)/shard_map/all_gather | solution.py:195
  217.5 19.1 %multiply_convert_fusion.1 = (bf16[2048,768]{1,0:T(8,128)(2,1)}, f32[2048,768]{1,0:T(8,128)}, f32[2048,768]{1,0:T(8,128)}) fusion(f32[2048,768]{1,0:T(8,128)} %fusion.74, bf16[2048,768]{1,0:T(8,128)(2,1)} %all-gather.12.cloned.1.call-done, bf16[768,768]{1,0:T(8,128)(2,1)} %all-gather.16.cloned.1.call-done), kind=kOutput, calls=%fused_computation.5 | convolution fusion | flops 2519728128 | bytes 26345472 | tf_op jit(solution)/shard_map/dot_general | solution.py:52
  236.6 23.4 %all-gather.18.cloned.1.call-done = bf16[768,768]{0,1:T(8,128)(2,1)} async-done(((bf16[768,96]{0,1:T(8,128)(2,1)}), bf16[768,768]{0,1:T(8,128)(2,1)}) %all-gather.18.cloned.1.call-update) | async-done | bytes 1179664 | tf_op jit(solution)/shard_map/all_gather | solution.py:196
  260.0 7.5 fusion.75
  267.7 1.7 fusion.73
  269.4 55.4 %reduce-scatter.17.cloned.1.call-done = f32[512,768]{1,0:T(8,128)} async-done(((f32[2048,768]{1,0:T(8,128)}), f32[512,768]{1,0:T(8,128)}) %reduce-scatter.17.cloned.1.call-update) | async-done | bytes 1572880 | tf_op jit(solution)/shard_map/reduce_scatter | solution.py:225
  324.8 2.5 fusion.67
  328.3 1.6 fusion.66
  329.9 1.1 copy-done.5
  331.0 1.1 add_convert_fusion.3
  332.6 28.2 %all-gather.20.cloned.1.call-done = bf16[2048,768]{1,0:T(8,128)(2,1)} async-done(((bf16[512,768]{1,0:T(8,128)(2,1)}), bf16[2048,768]{1,0:T(8,128)(2,1)}) %all-gather.20.cloned.1.call-update) | async-done | bytes 3145744 | tf_op jit(solution)/shard_map/all_gather | solution.py:236
  360.8 10.1 %multiply_convert_fusion = (bf16[2048,768]{1,0:T(8,128)(2,1)S(1)}, bf16[2048,768]{1,0:T(8,128)(2,1)S(1)}) fusion(f32[2048,768]{1,0:T(8,128)} %get-tuple-element.198, f32[2048,768]{1,0:T(8,128)} %fusion.74, f32[2048,768]{1,0:T(8,128)} %get-tuple-element.209, bf16[2048,768]{1,0:T(8,128)(2,1)} %all-gather.20.cloned.1.call-done, ...), kind=kOutput, calls=%fused_computation.3 | convolution fusion | flops 2444230656 | bytes 29491200 | tf_op jit(solution)/shard_map/dot_general | solution.py:35
  371.0 2.7 fusion.76
  373.6 4.6 convolution_add_fusion
  378.3 58.5 %reduce-scatter.19.cloned.1.call-done = f32[512,768]{1,0:T(8,128)} async-done(((f32[2048,768]{1,0:T(8,128)}), f32[512,768]{1,0:T(8,128)}) %reduce-scatter.19.cloned.1.call-update) | async-done | bytes 1572880 | tf_op jit(solution)/shard_map/reduce_scatter | solution.py:243
  436.7 3.3 multiply_reduce_fusion.1
  440.7 1.1 copy-done.11
  441.9 2.3 fusion.29
  444.4 3.5 convolution_convert_fusion.1
  447.9 2.3 copy.144
  450.2 2.4 reshape.294
  452.7 2.4 multiply_reduce_fusion
  456.2 1.2 multiply_bitcast_fusion
  458.0 1.2 fusion.19
  459.5 2.2 copy.150
  461.7 1.4 copy-done.16
  463.1 4.9 fusion.8
  468.3 1.6 copy-done.40
  469.9 6.0 fusion.77
  476.0 6.1 fusion.78
  482.1 6.9 fusion.79
  489.5 2.7 reshape.313
  492.3 2.3 copy.173
  495.0 49.0 %reduce-scatter.21.cloned.1.call-done = f32[768,576]{0,1:T(8,128)} async-done(((f32[768,2304]{0,1:T(8,128)}), f32[768,576]{0,1:T(8,128)}) %reduce-scatter.21.cloned.1.call-update) | async-done | bytes 1769488 | tf_op jit(solution)/shard_map/reduce_scatter | solution.py:262
  543.9 2.8 copy.171
  550.2 66.8 %reduce-scatter.25.cloned.1.call-done = f32[96,768]{1,0:T(8,128)} async-done(((f32[768,768]{1,0:T(8,128)}), f32[96,768]{1,0:T(8,128)}) %reduce-scatter.25.cloned.1.call-update) | async-done | bytes 294928 | tf_op jit(solution)/shard_map/reduce_scatter | solution.py:269
  617.1 2.2 multiply_subtract_fusion.3
  619.2 70.0 %reduce-scatter.27.cloned.1.call-done = f32[96,768]{1,0:T(8,128)} async-done(((f32[768,768]{1,0:T(8,128)}), f32[96,768]{1,0:T(8,128)}) %reduce-scatter.27.cloned.1.call-update) | async-done | bytes 294928 | tf_op jit(solution)/shard_map/reduce_scatter | solution.py:270
  689.2 2.2 multiply_subtract_fusion.2
  691.4 70.0 %reduce-scatter.29.cloned.1.call-done = f32[768,96]{0,1:T(8,128)} async-done(((f32[768,768]{0,1:T(8,128)}), f32[768,96]{0,1:T(8,128)}) %reduce-scatter.29.cloned.1.call-update) | async-done | bytes 294928 | tf_op jit(solution)/shard_map/reduce_scatter | solution.py:271
  761.4 2.2 multiply_subtract_fusion.1
  763.6 6.0 add_add_fusion.2
  769.6 92.9 %reduce-scatter.35.cloned.1.call-done = f32[96,1]{1,0:T(8,128)} async-done(((f32[3072,1]{1,0:T(8,128)}), f32[96,1]{1,0:T(8,128)}) %reduce-scatter.35.cloned.1.call-update) | async-done | bytes 400
  864.0 63.8 %reduce-scatter.33.cloned.1.call-done = f32[96,192]{1,0:T(8,128)} async-done(((f32[768,192]{1,0:T(8,128)}), f32[96,192]{1,0:T(8,128)}) %reduce-scatter.33.cloned.1.call-update) | async-done | bytes 73744
  931.0 66.8 %reduce-scatter.31.cloned.1.call-done = f32[96,576]{1,0:T(8,128)} async-done(((f32[768,576]{1,0:T(8,128)}), f32[96,576]{1,0:T(8,128)}) %reduce-scatter.31.cloned.1.call-update) | async-done | bytes 221200
  997.9 1.1 copy.172
  (184 shorter events, 23.0 us)
Async XLA Ops:
  7.2 260.5 %copy-start = (bf16[4,32,768]{2,1,0:T(8,128)(2,1)S(1)}, bf16[4,32,768]{2,1,0:T(8,128)(2,1)}, u32[]{:S(2)}) copy-start(bf16[4,32,768]{2,1,0:T(8,128)(2,1)} %param.30) | copy-start | bytes 589828
  7.2 36.9 %copy-start.25 = (f32[96,192]{1,0:T(8,128)S(1)}, f32[96,192]{1,0:T(8,128)}, u32[]{:S(2)}) copy-start(f32[96,192]{1,0:T(8,128)} %param.33) | copy-start | bytes 221188
  7.2 69.0 %copy-start.17 = (f32[96,768]{1,0:T(8,128)S(1)}, f32[96,768]{1,0:T(8,128)}, u32[]{:S(2)}) copy-start(f32[96,768]{1,0:T(8,128)} %param.35) | copy-start | bytes 884740
  7.2 69.8 %copy-start.34 = (s32[4,32]{1,0:T(4,128)S(1)}, s32[4,32]{1,0:T(4,128)}, u32[]{:S(2)}) copy-start(s32[4,32]{1,0:T(4,128)} %param.29) | copy-start | bytes 1540
  7.3 69.9 %copy-start.36 = (s32[4]{0:T(128)S(1)}, s32[4]{0:T(128)}, u32[]{:S(2)}) copy-start(s32[4]{0:T(128)} %param.28) | copy-start | bytes 52
  7.3 116.5 %all-gather.8.cloned.1.call-start = ((), (), s32[]{:S(2)}) async-start(), calls=%async_computation.10 | async-start | bytes 4423680 | tf_op jit(solution)/shard_map/all_gather | solution.py:206
  8.4 68.9 %copy-start.37 = (f32[1,96]{1,0:T(1,128)S(1)}, f32[1,96]{1,0:T(1,128)}, u32[]{:S(2)}) copy-start(f32[1,96]{1,0:T(1,128)} %param.34) | copy-start | bytes 1156
  42.8 75.7 %copy-start.33 = (s32[4,32]{1,0:T(4,128)S(1)}, s32[4,32]{1,0:T(4,128)}, u32[]{:S(2)}) copy-start(s32[4,32]{1,0:T(4,128)} %param.27) | copy-start | bytes 1540
  44.1 79.1 %copy-start.22 = (bf16[512,768]{1,0:T(8,128)(2,1)S(1)}, bf16[512,768]{1,0:T(8,128)(2,1)}, u32[]{:S(2)}) copy-start(bf16[512,768]{1,0:T(8,128)(2,1)} %param.25) | copy-start | bytes 2359300
  44.1 95.6 %all-gather.10.cloned.1.call-start = ((), (), s32[]{:S(2)}) async-start(), calls=%async_computation.11 | async-start | bytes 1474560 | tf_op jit(solution)/shard_map/all_gather | solution.py:207
  76.2 72.2 %all-gather.14.cloned.1.call-start = ((), (), s32[]{:S(2)}) async-start(), calls=%async_computation.13 | async-start | bytes 1327104 | tf_op jit(solution)/shard_map/all_gather | solution.py:194
  76.9 96.9 %all-gather.12.cloned.1.call-start = ((), (), s32[]{:S(2)}) async-start(), calls=%async_computation.12 | async-start | bytes 3932160 | tf_op jit(solution)/shard_map/all_gather | solution.py:223
  123.8 4.3 copy-start.23
  134.7 1.1 copy-start.14
  135.8 1.7 copy-start.6
  135.8 1.7 copy-start.8
  135.8 1.7 copy-start.15
  142.3 1.1 copy-start.2
  144.7 72.8 %all-gather.16.cloned.1.call-start = ((), (), s32[]{:S(2)}) async-start(), calls=%async_computation.14 | async-start | bytes 1327104 | tf_op jit(solution)/shard_map/all_gather | solution.py:195
  146.4 113.6 %all-gather.18.cloned.1.call-start = ((), (), s32[]{:S(2)}) async-start(), calls=%async_computation.15 | async-start | bytes 1327104 | tf_op jit(solution)/shard_map/all_gather | solution.py:196
  148.1 176.7 %reduce-scatter.17.cloned.1.call-start = ((), (), s32[]{:S(2)}) async-start(), calls=%async_computation.16 | async-start | bytes 7864320 | tf_op jit(solution)/shard_map/reduce_scatter | solution.py:225
  267.5 93.3 %all-gather.20.cloned.1.call-start = ((), (), s32[]{:S(2)}) async-start(), calls=%async_computation.17 | async-start | bytes 3932160 | tf_op jit(solution)/shard_map/all_gather | solution.py:236
  324.8 2.8 copy-start.4
  329.9 1.1 copy-start.5
  332.1 104.6 %reduce-scatter.19.cloned.1.call-start = ((), (), s32[]{:S(2)}) async-start(), calls=%async_computation.18 | async-start | bytes 7864320 | tf_op jit(solution)/shard_map/reduce_scatter | solution.py:243
  360.8 10.1 %copy-start.41 = (bf16[768,768]{1,0:T(8,128)(2,1)S(1)}, bf16[768,768]{1,0:T(8,128)(2,1)}, u32[]{:S(2)}) copy-start(bf16[768,768]{1,0:T(8,128)(2,1)} %all-gather.14.cloned.1.call-done) | copy-start | bytes 3538948
  370.9 2.7 copy-start.44
  370.9 2.7 copy-start.43
  370.9 2.7 copy-start.42
  378.2 114.0 %reduce-scatter.23.cloned.1.call-start = ((), (), s32[]{:S(2)}) async-start(), calls=%async_computation.20 | async-start | bytes 2949120 | tf_op jit(solution)/shard_map/reduce_scatter | solution.py:263
  436.7 3.3 copy-start.3
  440.0 1.8 copy-start.13
  440.7 1.1 copy-start.11
  444.2 99.7 %reduce-scatter.21.cloned.1.call-start = ((), (), s32[]{:S(2)}) async-start(), calls=%async_computation.19 | async-start | bytes 8847360 | tf_op jit(solution)/shard_map/reduce_scatter | solution.py:262
  455.1 1.1 copy-start.9
  456.2 1.2 copy-start.7
  456.2 1.7 copy-start.10
  459.5 3.7 copy-start.24
  461.7 1.4 copy-start.16
  468.0 1.9 copy-start.40
  468.0 149.0 %reduce-scatter.25.cloned.1.call-start = ((), (), s32[]{:S(2)}) async-start(), calls=%async_computation.21 | async-start | bytes 2654208 | tf_op jit(solution)/shard_map/reduce_scatter | solution.py:269
  476.0 213.3 %reduce-scatter.27.cloned.1.call-start = ((), (), s32[]{:S(2)}) async-start(), calls=%async_computation.22 | async-start | bytes 2654208 | tf_op jit(solution)/shard_map/reduce_scatter | solution.py:270
  482.1 279.3 %reduce-scatter.29.cloned.1.call-start = ((), (), s32[]{:S(2)}) async-start(), calls=%async_computation.23 | async-start | bytes 2654208 | tf_op jit(solution)/shard_map/reduce_scatter | solution.py:271
  489.1 373.4 %reduce-scatter.35.cloned.1.call-start = ((), (), s32[]{:S(2)}) async-start(), calls=%async_computation.26 | async-start | bytes 1622016
  492.2 435.6 %reduce-scatter.33.cloned.1.call-start = ((), (), s32[]{:S(2)}) async-start(), calls=%async_computation.25 | async-start | bytes 884736
  494.6 52.2 %copy-start.21 = (f32[96,576]{1,0:T(8,128)S(1)}, f32[96,576]{1,0:T(8,128)}, u32[]{:S(2)}) copy-start(f32[96,576]{1,0:T(8,128)} %param.32) | copy-start | bytes 663556
  494.6 53.8 %copy-start.29 = (f32[96,576]{1,0:T(8,128)S(1)}, f32[96,576]{1,0:T(8,128)}, u32[]{:S(2)}) copy-start(f32[96,576]{1,0:T(8,128)} %param.44) | copy-start | bytes 663556
  494.6 54.0 %copy-start.30 = (f32[96,576]{1,0:T(8,128)S(1)}, f32[96,576]{1,0:T(8,128)}, u32[]{:S(2)}) copy-start(f32[96,576]{1,0:T(8,128)} %param.38) | copy-start | bytes 663556
  494.6 54.1 %copy-start.31 = (f32[96,192]{1,0:T(8,128)S(1)}, f32[96,192]{1,0:T(8,128)}, u32[]{:S(2)}) copy-start(f32[96,192]{1,0:T(8,128)} %param.45) | copy-start | bytes 221188
  494.7 54.8 %copy-start.32 = (f32[96,192]{1,0:T(8,128)S(1)}, f32[96,192]{1,0:T(8,128)}, u32[]{:S(2)}) copy-start(f32[96,192]{1,0:T(8,128)} %param.39) | copy-start | bytes 221188
  494.7 122.4 %copy-start.18 = (f32[96,768]{1,0:T(8,128)S(1)}, f32[96,768]{1,0:T(8,128)}, u32[]{:S(2)}) copy-start(f32[96,768]{1,0:T(8,128)} %param.35) | copy-start | bytes 884740
  494.7 503.2 %reduce-scatter.31.cloned.1.call-start = ((), (), s32[]{:S(2)}) async-start(), calls=%async_computation.24 | async-start | bytes 2211840
  546.7 142.5 %copy-start.19 = (f32[96,768]{1,0:T(8,128)S(1)}, f32[96,768]{1,0:T(8,128)}, u32[]{:S(2)}) copy-start(f32[96,768]{1,0:T(8,128)} %param.36) | copy-start | bytes 884740
  546.8 214.6 %copy-start.20 = (f32[768,96]{0,1:T(8,128)S(1)}, f32[768,96]{0,1:T(8,128)}, u32[]{:S(2)}) copy-start(f32[768,96]{0,1:T(8,128)} %param.37) | copy-start | bytes 884740
  550.2 213.3 %copy-start.12 = (f32[512,768]{1,0:T(8,128)S(1)}, f32[512,768]{1,0:T(8,128)}, u32[]{:S(2)}) copy-start(f32[512,768]{1,0:T(8,128)} %copy-done.11) | copy-start | bytes 4718596
  763.5 99.9 %copy-start.38 = (f32[1,96]{1,0:T(1,128)S(1)}, f32[1,96]{1,0:T(1,128)}, u32[]{:S(2)}) copy-start(f32[1,96]{1,0:T(1,128)} %param.46) | copy-start | bytes 1156
  763.5 99.9 %copy-start.39 = (f32[1,96]{1,0:T(1,128)S(1)}, f32[1,96]{1,0:T(1,128)}, u32[]{:S(2)}) copy-start(f32[1,96]{1,0:T(1,128)} %param.40) | copy-start | bytes 1156
  763.5 165.2 %copy-start.26 = (f32[96,192]{0,1:T(8,128)S(1)}, f32[96,192]{0,1:T(8,128)}, u32[]{:S(2)}) copy-start(f32[96,192]{0,1:T(8,128)} %copy.158) | copy-start | bytes 221188
  763.6 165.2 %copy-start.27 = (f32[96,192]{0,1:T(8,128)S(1)}, f32[96,192]{0,1:T(8,128)}, u32[]{:S(2)}) copy-start(f32[96,192]{0,1:T(8,128)} %copy.154) | copy-start | bytes 221188
  763.6 165.2 %copy-start.28 = (f32[96,192]{0,1:T(8,128)S(1)}, f32[96,192]{0,1:T(8,128)}, u32[]{:S(2)}) copy-start(f32[96,192]{0,1:T(8,128)} %copy.152) | copy-start | bytes 221188
  763.6 238.2 %copy-start.1 = (bf16[4,32,768]{2,1,0:T(8,128)(2,1)S(1)}, bf16[4,32,768]{2,1,0:T(8,128)(2,1)}, u32[]{:S(2)}) copy-start(bf16[4,32,768]{2,1,0:T(8,128)(2,1)} %param.30) | copy-start | bytes 589828
  863.4 138.4 %copy-start.35 = (f32[1,96]{1,0:T(1,128)}, f32[1,96]{1,0:T(1,128)S(1)}, u32[]{:S(2)}) copy-start(f32[1,96]{1,0:T(1,128)S(1)} %copy.176) | copy-start | bytes 1156
Sparse Core Ops, SparseCore 0:
  44.2 31.5 all-gather.7
  78.0 17.6 all-gather.9
  98.4 41.0 all-gather.13
  144.8 28.9 all-gather.11
  176.4 41.0 all-gather.15
  220.1 39.8 all-gather.17
  267.6 57.1 reduce-scatter.16
  332.2 28.5 all-gather.19
  378.3 58.3 reduce-scatter.18
  444.3 33.0 reduce-scatter.22
  480.2 63.7 reduce-scatter.20
  547.9 69.1 reduce-scatter.24
  621.1 68.0 reduce-scatter.26
  693.2 68.1 reduce-scatter.28
  766.5 96.0 reduce-scatter.34
  866.3 61.4 reduce-scatter.32
  932.0 65.8 reduce-scatter.30
where the time goes:
time: 1020 us; the launch traced here: 1010 us
  waiting for transfers between devices  707 us (69%)
  blocking collectives  105 us (10%)
  matrix products  103 us (10%)
  local copies, waits for them, and re-layouts  48.5 us (5%)
  other arithmetic  27.1 us (3%)
  between operations  15.9 us (2%)
    unnamed x20, waiting for transfers between devices  224 us
    reduce_scatter x1, waiting for transfers between devices, shards(): lax.psum_scatter(value_part, 'dp', scatter_dimension=0, tiled=True)  70 us
    reduce_scatter x1, waiting for transfers between devices, shards(): lax.psum_scatter(down_part, 'dp', scatter_dimension=1, tiled=True)  70 us
    reduce_scatter x1, waiting for transfers between devices, shards(): lax.psum_scatter(gate_part, 'dp', scatter_dimension=0, tiled=True)  66.8 us
    reduce_scatter x1, waiting for transfers between devices, shards(): lax.psum_scatter(right_transposed(gate_part, gate_full) + right_transpose...  58.5 us
    reduce_scatter x1, waiting for transfers between devices, shards(): lax.psum_scatter(jnp.dot(hidden, down_full, preferred_element_type=jnp.fl...  55.4 us
    reduce_scatter x1, waiting for transfers between devices, shards(): lax.psum_scatter(attend_grad, 'mp', scatter_dimension=1, tiled=True)  49 us
    unnamed x1, blocking collectives  39.8 us
  transfers between devices with their start and end apart: 17, of which 13 were waited for; matrix products, arithmetic and copies ran while one was open for 13% of the time, Pallas kernels for 0%

commit v1 on v0

v1 whole, which is shorter than its diff:
```python
from functools import partial

import jax
import jax.numpy as jnp
from jax import lax
from jax.sharding import PartitionSpec as P

HEADS = 12
HEAD_DIM = 64


beta_one = 0.9
beta_two = 0.999
peak_rate = 1.0
warm_steps = 4.0
total_steps = 100.0
decay_rate = 0.01
adam_eps = 1e-08
norm_eps = 1e-05


def layer_norm(row_data, gain_row, shift_row):
    centered = row_data - jnp.mean(row_data, axis=-1, keepdims=True)
    spread = jnp.mean(centered * centered, axis=-1, keepdims=True)
    return centered * lax.rsqrt(spread + norm_eps) * gain_row + shift_row


def alibi_table(head_count, seq_len):
    slopes = jnp.exp2(-8.0 * jnp.arange(1, head_count + 1, dtype=jnp.float32) / head_count)
    places = jnp.arange(seq_len, dtype=jnp.float32)
    return slopes[:, None, None] * jnp.abs(places[:, None] - places[None, :])


def dot_nn(left_op, right_op):
    return lax.dot_general(
        left_op, right_op, (((1,), (0,)), ((), ())), preferred_element_type=jnp.float32
    )


def dot_nt(left_op, right_op):
    return lax.dot_general(
        left_op, right_op, (((1,), (1,)), ((), ())), preferred_element_type=jnp.float32
    )


def dot_tn(left_op, right_op):
    return lax.dot_general(
        left_op, right_op, (((0,), (0,)), ((), ())), preferred_element_type=jnp.float32
    )


def flip(block, axis, bits):
    size = lax.axis_size(axis)
    return lax.ppermute(block, axis, [(i, i ^ bits) for i in range(size)])


def flip_core(block):
    return flip(block, "mp", 1)


def flip_x(block):
    return flip(block, "mp", 2)


def flip_y(block):
    return flip(block, "dp", 1)


def z_groups():
    size = lax.axis_size("dp")
    return [list(range(low, size, 2)) for low in range(2)]


def place(total, block, at):
    return lax.dynamic_update_slice(total, block[None], (at,) + (0,) * block.ndim)


def gather_z(block):
    z_size = lax.axis_size("dp") // 2
    if z_size != 4:
        return lax.all_gather(block, "dp", axis=0, axis_index_groups=z_groups())
    z_at = lax.axis_index("dp") // 2
    parts = [block] + [flip(block, "dp", 2 * k) for k in range(1, 4)]
    total = jnp.zeros((4,) + block.shape, block.dtype)
    for k, part in enumerate(parts):
        total = place(total, part, z_at ^ k)
    return total


def join_y(mine, other):
    y_at = lax.axis_index("dp") % 2
    z_size, rows, columns = mine.shape
    total = jnp.zeros((z_size, 2, rows, columns), mine.dtype)
    total = lax.dynamic_update_slice(total, mine[:, None], (0, y_at, 0, 0))
    total = lax.dynamic_update_slice(total, other[:, None], (0, 1 - y_at, 0, 0))
    return total.reshape(z_size * 2 * rows, columns)


def gather_zyx(block):
    along_z = gather_z(block)
    whole = join_y(along_z, flip_y(along_z))
    return whole, flip_x(whole)


def gather_zxy(block):
    along_z = gather_z(block)
    along_x = jnp.stack([along_z, flip_x(along_z)])
    other = flip_y(along_x)
    return join_y(along_x[0], other[0]), join_y(along_x[1], other[1])


def sum_z(parts):
    z_size = lax.axis_size("dp") // 2
    if z_size != 4:
        return lax.psum_scatter(
            parts.astype(jnp.float32), "dp", scatter_dimension=0, axis_index_groups=z_groups()
        )
    z_at = lax.axis_index("dp") // 2
    total = lax.dynamic_index_in_dim(parts, z_at, 0, keepdims=False).astype(jnp.float32)
    for k in range(1, 4):
        sent = lax.dynamic_index_in_dim(parts, z_at ^ k, 0, keepdims=False)
        total = total + flip(sent, "dp", 2 * k).astype(jnp.float32)
    return total


def add_low(left_op, right_op):
    return (left_op.astype(jnp.float32) + right_op.astype(jnp.float32)).astype(jnp.bfloat16)


def by_feature(partial_sum):
    size = lax.axis_size("dp")
    features, columns = partial_sum.shape
    return partial_sum.astype(jnp.bfloat16).reshape(size // 2, 2, features // size, columns)


def pick_y(parts, y_at):
    axis = parts.ndim - 3
    return lax.dynamic_index_in_dim(parts, y_at, axis, keepdims=False)


def scatter_xyz(mine, other):
    y_at = lax.axis_index("dp") % 2
    along_x = add_low(by_feature(mine), flip_x(by_feature(other)))
    along_y = add_low(pick_y(along_x, y_at), flip_y(pick_y(along_x, 1 - y_at)))
    return sum_z(along_y)


def scatter_yxz(mine, other):
    y_at = lax.axis_index("dp") % 2
    both = jnp.stack([by_feature(mine), by_feature(other)])
    along_y = add_low(pick_y(both, y_at), flip_y(pick_y(both, 1 - y_at)))
    along_x = add_low(along_y[0], flip_x(along_y[1]))
    return sum_z(along_x)


def gelu_parts(gated):
    below = 0.5 * (1.0 + lax.erf(gated * 0.7071067811865476))
    density = 0.3989422804014327 * jnp.exp(-0.5 * gated * gated)
    return gated * below, below + gated * density


def norm_stats(row_data):
    centered = row_data - jnp.mean(row_data, axis=-1, keepdims=True)
    spread = jnp.mean(centered * centered, axis=-1, keepdims=True)
    inverse = lax.rsqrt(spread + norm_eps)
    return centered * inverse, inverse


def norm_back(xhat, inverse, gain_row, incoming):
    scaled = incoming * gain_row
    inner = jnp.mean(scaled * xhat, axis=-1, keepdims=True)
    back = inverse * (scaled - jnp.mean(scaled, axis=-1, keepdims=True) - xhat * inner)
    return back, jnp.sum(incoming * xhat, axis=0), jnp.sum(incoming, axis=0)


def adamw_step(master, first, second, gradient, step_value, decay):
    step_rate = peak_rate * jnp.minimum(
        step_value / warm_steps, (total_steps - step_value) / (total_steps - warm_steps)
    )
    fix_one = 1.0 - jnp.power(jnp.float32(beta_one), step_value)
    fix_two = 1.0 - jnp.power(jnp.float32(beta_two), step_value)
    moment = beta_one * first + (1.0 - beta_one) * gradient
    squares = beta_two * second + (1.0 - beta_two) * gradient * gradient
    updated = master - step_rate * (
        moment / fix_one / (jnp.sqrt(squares / fix_two) + adam_eps) + decay * master
    )
    return (moment, squares, updated)


def shards(
    hidden_rows,
    token_table,
    masked_positions,
    masked_counts,
    replace_rows,
    masked_cotangent,
    step_number,
    attend_master,
    merge_master,
    norms_master,
    gate_master,
    value_master,
    down_master,
    first_attend,
    first_merge,
    first_norms,
    first_gate,
    first_value,
    first_down,
    second_attend,
    second_merge,
    second_norms,
    second_gate,
    second_value,
    second_down,
):
    local_seqs, slot_count = masked_positions.shape
    local_rows, model_width = hidden_rows.shape
    length = local_rows // local_seqs
    slot_rows = local_seqs * slot_count
    dp_size = lax.axis_size("dp")
    mp_size = lax.axis_size("mp")
    core_at = lax.axis_index("mp") % 2
    low = jnp.bfloat16

    half_width = model_width // 2
    attend_low = attend_master.astype(low)
    attend_cut = attend_low.shape[1]
    packet = jnp.concatenate([attend_low, merge_master.astype(low)], axis=1)
    norms_z = gather_z(norms_master)
    first_packs = gather_zyx(packet[:, :half_width])
    second_packs = gather_zxy(packet[:, half_width:])
    norms_y = flip_y(norms_z)
    norms_own = join_y(norms_z.reshape(dp_size // 2, -1, 1), norms_y.reshape(dp_size // 2, -1, 1))
    norms_own = norms_own.reshape(1, model_width)
    norms_pair = jnp.concatenate([norms_own, flip_core(norms_own)], axis=0)
    norms_far = flip_x(norms_pair)
    x_at = lax.axis_index("mp") // 2
    norms = jnp.zeros((mp_size, model_width), jnp.float32)
    for far, pair in enumerate((norms_pair, norms_far)):
        for core in range(2):
            norms = place(norms, pair[core], 2 * (x_at ^ far) + (core_at ^ core))
    gate_full = gather_zyx(gate_master.astype(low))
    value_full = gather_zxy(value_master.astype(low))
    down_low = down_master.astype(low).T
    down_first = gather_zyx(down_low[:, :half_width])
    down_second = gather_zxy(down_low[:, half_width:])
    down_full = [jnp.concatenate([down_first[k], down_second[k]], axis=1) for k in range(2)]

    near = [jnp.concatenate([first_packs[k], second_packs[k]], axis=1) for k in range(2)]
    near = jnp.stack(near)
    far = flip_core(near)
    attend_parts = jnp.zeros((mp_size, model_width, model_width), low)
    for core, packs in enumerate((near, far)):
        for k in range(2):
            attend_parts = place(attend_parts, packs[k], 2 * (x_at ^ k) + (core_at ^ core))
    attend_full = (
        attend_parts[:, :, :attend_cut].transpose(1, 0, 2).reshape(model_width, 3 * model_width)
    )
    merge_full = (
        attend_parts[:, :, attend_cut:].transpose(1, 0, 2).reshape(model_width, model_width)
    )

    live_slots = jnp.arange(slot_count, dtype=jnp.int32)[None, :] < masked_counts[:, None]
    at_slot = masked_positions[:, :, None] == jnp.arange(length, dtype=jnp.int32)[None, None, :]
    place_bool = at_slot & live_slots[:, :, None]
    place_low = place_bool.astype(low)
    select_low = at_slot.astype(low)
    chosen = jnp.take(token_table, replace_rows.reshape(-1), axis=0).reshape(
        local_seqs, slot_count, model_width
    )
    swapped = jnp.einsum(
        "sjt,sjd->std", place_low, chosen, preferred_element_type=jnp.float32
    ).astype(low)
    replaced = jnp.any(place_bool, axis=1)[:, :, None]
    start_rows = jnp.where(
        replaced, swapped, hidden_rows.reshape(local_seqs, length, model_width)
    ).reshape(local_rows, model_width)

    def slot_low(rows):
        picked = jnp.einsum(
            "sjt,std->sjd",
            select_low,
            rows.reshape(local_seqs, length, -1),
            preferred_element_type=jnp.float32,
        )
        return picked.astype(low).reshape(slot_rows, -1)

    def slot_wide(rows):
        picked = jnp.einsum(
            "sjt,std->sjd",
            at_slot.astype(jnp.float32),
            rows.reshape(local_seqs, length, -1),
            precision=lax.Precision.HIGHEST,
        )
        return picked.reshape(slot_rows, -1)

    alibi = alibi_table(HEADS, length)
    scale = HEAD_DIM ** (-0.5)
    mixed = dot_nn(start_rows, attend_full).astype(low)
    heads_shape = (local_seqs, length, 3, HEADS, HEAD_DIM)
    queries, key_rows, value_rows = (
        mixed.reshape(heads_shape)[:, :, part].transpose(0, 2, 1, 3) for part in range(3)
    )
    scores = (
        jnp.einsum("bhse,bhte->bhst", queries, key_rows, preferred_element_type=jnp.float32) * scale
        - alibi
    )
    row_max = jnp.max(scores, axis=-1, keepdims=True)
    exp_scores = jnp.exp(scores - row_max)
    row_total = jnp.sum(exp_scores, axis=-1, keepdims=True)
    probs = (exp_scores / row_total).astype(low)
    attended = jnp.einsum("bhst,bhte->bhse", probs, value_rows, preferred_element_type=jnp.float32)
    attended_rows = attended.astype(low).transpose(0, 2, 1, 3).reshape(local_rows, model_width)
    first_sum = start_rows.astype(jnp.float32) + dot_nn(attended_rows, merge_full)
    first_hat, first_inverse = norm_stats(first_sum)
    normed = first_hat * norms[0] + norms[1]
    narrow = normed.astype(low)

    chip_rows = jnp.concatenate([narrow, flip_core(narrow)], axis=0)
    ffn_part = 0.0
    for k in range(2):
        gated = dot_nn(chip_rows, gate_full[k])
        valued = dot_nn(chip_rows, value_full[k])
        hidden = (gelu_parts(gated)[0] * valued).astype(low)
        ffn_part = ffn_part + dot_nt(hidden, down_full[k])
    ffn_out = ffn_part[:local_rows] + flip_core(ffn_part[local_rows:])
    second_sum = normed + ffn_out
    second_hat, second_inverse = norm_stats(second_sum)
    layer_output = (second_hat * norms[2] + norms[3]).astype(low)

    slot_cotangent = jnp.where(
        live_slots[:, :, None], masked_cotangent.astype(jnp.float32), 0.0
    ).reshape(slot_rows, model_width)
    slot_hat, slot_inverse = norm_stats(slot_wide(second_sum))
    second_back, gain_two_back, shift_two_back = norm_back(
        slot_hat, slot_inverse, norms[2], slot_cotangent
    )
    pulled = second_back.astype(low)
    slot_narrow = slot_low(narrow)
    sent = jnp.stack([pulled, slot_narrow])
    got = flip_core(sent)
    work_pull = jnp.concatenate([pulled, got[0]], axis=0)
    work_rows = jnp.concatenate([slot_narrow, got[1]], axis=0)
    gate_grads, value_grads, down_grads = [], [], []
    normed_part = 0.0
    for k in range(2):
        gated = dot_nn(work_rows, gate_full[k])
        valued = dot_nn(work_rows, value_full[k])
        gelu, slope = gelu_parts(gated)
        hidden = (gelu * valued).astype(low)
        hidden_back = dot_nn(work_pull, down_full[k])
        gate_back = (hidden_back * valued * slope).astype(low)
        value_back = (hidden_back * gelu).astype(low)
        down_grads.append(dot_tn(work_pull, hidden))
        gate_grads.append(dot_tn(work_rows, gate_back))
        value_grads.append(dot_tn(work_rows, value_back))
        normed_part = (
            normed_part + dot_nt(gate_back, gate_full[k]) + dot_nt(value_back, value_full[k])
        )
    gradient_gate = scatter_xyz(gate_grads[0], gate_grads[1])
    gradient_value = scatter_yxz(value_grads[0], value_grads[1])
    gradient_down = jnp.concatenate(
        [
            scatter_xyz(down_grads[0][:, :half_width], down_grads[1][:, :half_width]),
            scatter_yxz(down_grads[0][:, half_width:], down_grads[1][:, half_width:]),
        ],
        axis=1,
    ).T
    normed_back = normed_part[:slot_rows] + flip_core(normed_part[slot_rows:])
    slot_hat, slot_inverse = norm_stats(slot_wide(first_sum))
    first_back, gain_one_back, shift_one_back = norm_back(
        slot_hat, slot_inverse, norms[0], normed_back + second_back
    )
    branch_pull = first_back.astype(low)
    attended_back = dot_nt(branch_pull, merge_full).astype(low)
    slot_attended = slot_low(attended_rows)
    slot_start = slot_low(start_rows)

    slot_queries = jnp.einsum(
        "sjt,shte->shje", select_low, queries, preferred_element_type=jnp.float32
    ).astype(low)
    slot_alibi = alibi_table(HEADS, length)
    slopes = jnp.exp2(-8.0 * jnp.arange(1, HEADS + 1, dtype=jnp.float32) / HEADS)
    apart = jnp.abs(
        masked_positions[:, :, None] - jnp.arange(length, dtype=jnp.int32)[None, None, :]
    ).astype(jnp.float32)
    slot_alibi = slopes[None, :, None, None] * apart[:, None]
    scores = (
        jnp.einsum("bhse,bhte->bhst", slot_queries, key_rows, preferred_element_type=jnp.float32)
        * scale
        - slot_alibi
    )
    row_max = jnp.max(scores, axis=-1, keepdims=True)
    exp_scores = jnp.exp(scores - row_max)
    probs = exp_scores / jnp.sum(exp_scores, axis=-1, keepdims=True)
    heads_back = attended_back.reshape(local_seqs, slot_count, HEADS, HEAD_DIM).transpose(
        0, 2, 1, 3
    )
    probs_back = jnp.einsum(
        "bhse,bhte->bhst", heads_back, value_rows, preferred_element_type=jnp.float32
    )
    inner = jnp.sum(probs * probs_back, axis=-1, keepdims=True)
    scores_back = (probs * (probs_back - inner)).astype(low)
    queries_back = (
        jnp.einsum("bhst,bhte->bhse", scores_back, key_rows, preferred_element_type=jnp.float32)
        * scale
    ).astype(low)
    keys_back = (
        jnp.einsum("bhst,bhse->bhte", scores_back, slot_queries, preferred_element_type=jnp.float32)
        * scale
    ).astype(low)
    values_back = jnp.einsum(
        "bhst,bhse->bhte", probs.astype(low), heads_back, preferred_element_type=jnp.float32
    ).astype(low)
    queries_back = jnp.einsum(
        "sjt,shje->shte", select_low, queries_back, preferred_element_type=jnp.float32
    ).astype(low)
    mixed_back = jnp.stack(
        [part.transpose(0, 2, 1, 3) for part in (queries_back, keys_back, values_back)], axis=2
    ).reshape(local_rows, 3 * model_width)
    placed_back = jnp.einsum(
        "sjt,sjd->std",
        at_slot.astype(jnp.float32),
        first_back.reshape(local_seqs, slot_count, model_width),
        precision=lax.Precision.HIGHEST,
    ).reshape(local_rows, model_width)
    input_gradient = placed_back + dot_nt(mixed_back, attend_full)

    merge_cut = merge_master.shape[1]
    grads = []
    for core in range(2):
        for k in range(2):
            block = 2 * (x_at ^ k) + (core_at ^ core)
            attend_cols = lax.dynamic_slice_in_dim(mixed_back, block * attend_cut, attend_cut, 1)
            merge_cols = lax.dynamic_slice_in_dim(branch_pull, block * merge_cut, merge_cut, 1)
            grads.append(
                jnp.concatenate(
                    [dot_tn(start_rows, attend_cols), dot_tn(slot_attended, merge_cols)], axis=1
                )
            )
    got = flip_core(jnp.stack(grads[2:]).astype(low))
    grads = [grads[k] + got[k].astype(jnp.float32) for k in range(2)]
    packed = jnp.concatenate(
        [
            scatter_xyz(grads[0][:, :half_width], grads[1][:, :half_width]),
            scatter_yxz(grads[0][:, half_width:], grads[1][:, half_width:]),
        ],
        axis=1,
    )
    gradient_attend, gradient_merge = packed[:, :attend_cut], packed[:, attend_cut:]

    norm_parts = jnp.stack([gain_one_back, shift_one_back, gain_two_back, shift_two_back], axis=0)
    norm_parts = norm_parts.reshape(2, 2, model_width)

    def mine_of(parts, at, axis):
        return lax.dynamic_index_in_dim(parts, at, axis, keepdims=False)

    norm_parts = mine_of(norm_parts, core_at, 1) + flip_core(mine_of(norm_parts, 1 - core_at, 1))
    norm_parts = mine_of(norm_parts, x_at, 0) + flip_x(mine_of(norm_parts, 1 - x_at, 0))
    norm_parts = norm_parts.reshape(dp_size // 2, 2, 1, -1)
    y_at = lax.axis_index("dp") % 2
    norm_parts = mine_of(norm_parts, y_at, 1) + flip_y(mine_of(norm_parts, 1 - y_at, 1))
    gradient_norms = sum_z(norm_parts)

    step_value = step_number[0].astype(jnp.float32)
    moment_attend, squares_attend, updated_attend = adamw_step(
        attend_master, first_attend, second_attend, gradient_attend, step_value, decay_rate
    )
    moment_merge, squares_merge, updated_merge = adamw_step(
        merge_master, first_merge, second_merge, gradient_merge, step_value, decay_rate
    )
    moment_norms, squares_norms, updated_norms = adamw_step(
        norms_master, first_norms, second_norms, gradient_norms, step_value, 0.0
    )
    moment_gate, squares_gate, updated_gate = adamw_step(
        gate_master, first_gate, second_gate, gradient_gate, step_value, decay_rate
    )
    moment_value, squares_value, updated_value = adamw_step(
        value_master, first_value, second_value, gradient_value, step_value, decay_rate
    )
    moment_down, squares_down, updated_down = adamw_step(
        down_master, first_down, second_down, gradient_down, step_value, decay_rate
    )
    return (
        layer_output,
        input_gradient,
        gradient_attend,
        gradient_merge,
        gradient_norms,
        gradient_gate,
        gradient_value,
        gradient_down,
        moment_attend,
        moment_merge,
        moment_norms,
        moment_gate,
        moment_value,
        moment_down,
        squares_attend,
        squares_merge,
        squares_norms,
        squares_gate,
        squares_value,
        squares_down,
        updated_attend,
        updated_merge,
        updated_norms,
        updated_gate,
        updated_value,
        updated_down,
    )


def solution(mesh):
    return jax.shard_map(
        shards,
        mesh=mesh,
        in_specs=(
            P(("dp", "mp"), None),
            P(),
            P(("dp", "mp"), None),
            P(("dp", "mp")),
            P(("dp", "mp"), None),
            P(("dp", "mp"), None, None),
            P(),
            P("dp", "mp"),
            P("dp", "mp"),
            P("mp", "dp"),
            P("dp", "mp"),
            P("dp", "mp"),
            P("mp", "dp"),
            P("dp", "mp"),
            P("dp", "mp"),
            P("mp", "dp"),
            P("dp", "mp"),
            P("dp", "mp"),
            P("mp", "dp"),
            P("dp", "mp"),
            P("dp", "mp"),
            P("mp", "dp"),
            P("dp", "mp"),
            P("dp", "mp"),
            P("mp", "dp"),
        ),
        out_specs=(
            P(("dp", "mp"), None),
            P(("dp", "mp"), None),
            P("dp", "mp"),
            P("dp", "mp"),
            P("mp", "dp"),
            P("dp", "mp"),
            P("dp", "mp"),
            P("mp", "dp"),
            P("dp", "mp"),
            P("dp", "mp"),
            P("mp", "dp"),
            P("dp", "mp"),
            P("dp", "mp"),
            P("mp", "dp"),
            P("dp", "mp"),
            P("dp", "mp"),
            P("mp", "dp"),
            P("dp", "mp"),
            P("dp", "mp"),
            P("mp", "dp"),
            P("dp", "mp"),
            P("dp", "mp"),
            P("mp", "dp"),
            P("dp", "mp"),
            P("dp", "mp"),
            P("mp", "dp"),
        ),
        check_vma=False,
    )
```

time: 1020 us -> 396 us (0.39)
  waiting for transfers between devices: 707 us -> 91.1 us
  blocking collectives: 105 us -> 0 us
  starting transfers between devices: 1.96 us -> 89.5 us
  local copies, waits for them, and re-layouts: 48.5 us -> 79.6 us
  matrix products: 103 us -> 79.4 us
  other arithmetic: 27.1 us -> 47.6 us
  between operations: 15.9 us -> 4 us
    reduce_scatter x7 -> x0, waiting for transfers between devices: 370 us -> none  [the longest x1 70 us: shards(): lax.psum_scatter(value_part, 'dp', scatter_dimension=0, tiled=True)]
    unnamed x20 -> x0, waiting for transfers between devices: 224 us -> none
    all_gather x7 -> x0, waiting for transfers between devices: 113 us -> none  [the longest x1 36.2 us: shards(): lax.all_gather(value_master.astype(jnp.bfloat16), 'dp', axis=0, tiled=True)]
    ppermute x0 -> x78, waiting for transfers between devices: none -> 91.1 us  [flip(): return lax.ppermute(block, axis, [(i, i ^ bits) for i in range(size)])]
    ppermute x0 -> x78, starting transfers between devices: none -> 89.5 us  [flip(): return lax.ppermute(block, axis, [(i, i ^ bits) for i in range(size)])]
    all_gather x2 -> x0, blocking collectives: 65.5 us -> none  [the longest x1 34.4 us: shards(): lax.all_gather(attend_master.astype(jnp.bfloat16), 'dp', axis=0, tiled=True)]
    unnamed x1 -> x0, blocking collectives: 39.8 us -> none
    dot_general x22 -> x45, matrix products: 103 us -> 78.8 us  [the longest x8 24.2 us: dot_nt(): lax.dot_general(left_op, right_op, (((1,), (1,)), ((), ())), preferred_el...]
  transfers between devices with their start and end apart: 17 -> 78, of which waited for: 13 -> 33; matrix products, arithmetic and copies ran while one was open for 13% -> 41% of each run, Pallas kernels for 0% -> 0%
where the time goes in v1:
time: 396 us; the launch traced here: 391 us
  waiting for transfers between devices  91.1 us (23%)
  starting transfers between devices  89.5 us (23%)
  local copies, waits for them, and re-layouts  79.6 us (20%)
  matrix products  79.4 us (20%)
  other arithmetic  47.6 us (12%)
  between operations  4 us (1%)
    ppermute x78, waiting for transfers between devices, flip(): return lax.ppermute(block, axis, [(i, i ^ bits) for i in range(size)])  91.1 us
    ppermute x78, starting transfers between devices, flip(): return lax.ppermute(block, axis, [(i, i ^ bits) for i in range(size)])  89.5 us
    dot_general x8, matrix products, dot_nt(): lax.dot_general(left_op, right_op, (((1,), (1,)), ((), ())), preferred_el...  24.2 us
    dot_general x10, matrix products, dot_nn(): lax.dot_general(left_op, right_op, (((1,), (0,)), ((), ())), preferred_el...  18.6 us
    dot_general x14, matrix products, dot_tn(): lax.dot_general(left_op, right_op, (((0,), (0,)), ((), ())), preferred_el...  14.8 us
    unnamed x192, local copies, waits for them, and re-layouts  12.2 us
    dynamic_update_slice x33, local copies, waits for them, and re-layouts, place(): lax.dynamic_update_slice(total, block[None], (at,) + (0,) * block.ndim)  10.6 us
    convert_element_type x12, other arithmetic, add_low(): (left_op.astype(jnp.float32) + right_op.astype(jnp.float32)).astype(jnp.b...  8.93 us
  transfers between devices with their start and end apart: 78, of which 33 were waited for; matrix products, arithmetic and copies ran while one was open for 41% of the time, Pallas kernels for 0%

profile of v1, /device:TPU:0, one launch (start us, length us, event | category | flops | bytes accessed | tf_op | source)
XLA Modules:
  0.0 391.2 jit_solution(7488716604148881933)
XLA Ops:
  2.5 3.0 collective-permute-start.22
  5.5 2.6 collective-permute-start.23
  9.0 3.5 collective-permute-start.12
  14.7 4.7 %gather_fusion = bf16[128,768]{1,0:T(8,128)(2,1)S(1)} fusion(bf16[4096,768]{1,0:T(8,128)(2,1)} %param.26, s32[1024]{0:T(1024)S(1)} %pad_clamp_fusion), kind=kCustom, calls=%fused_computation | custom fusion | bytes 393728 | tf_op jit(solution)/shard_map/jit(_take)/gather | solution.py:269
  25.3 3.5 collective-permute-done.13
  39.0 4.5 %collective-permute-done.32 = bf16[96,384]{1,0:T(8,128)(2,1)S(1)} collective-permute-done((bf16[96,384]{1,0:T(8,128)(2,1)S(1)}, bf16[96,384]{1,0:T(8,128)(2,1)S(1)}, u32[]{:S(2)}, u32[]{:S(2)}) %collective-permute-start.32) | collective-permute-done | bytes 73760 | tf_op jit(solution)/shard_map/ppermute | solution.py:54
  46.3 2.1 collective-permute-done.4
  49.9 2.1 collective-permute-done.5
  52.0 2.6 collective-permute-done.6
  58.0 2.1 collective-permute-done.1
  62.5 1.9 collective-permute-start.28
  68.0 2.0 collective-permute-start.34
  70.1 2.3 collective-permute-done.29
  78.8 2.4 collective-permute-done.7
  81.3 2.0 collective-permute-start.8
  83.3 2.5 collective-permute-done.3
  86.5 9.7 %collective-permute-done.35 = bf16[2,4,96,384]{3,2,1,0:T(8,128)(2,1)S(1)} collective-permute-done((bf16[2,4,96,384]{3,2,1,0:T(8,128)(2,1)S(1)}, bf16[2,4,96,384]{3,2,1,0:T(8,128)(2,1)S(1)}, u32[]{:S(2)}, u32[]{:S(2)}) %collective-permute-start.35) | collective-permute-done | bytes 589856 | tf_op jit(solution)/shard_map/ppermute | solution.py:54
  96.6 6.0 %collective-permute-done.8 = bf16[2,4,96,384]{3,2,1,0:T(8,128)(2,1)S(1)} collective-permute-done((bf16[2,4,96,384]{3,2,1,0:T(8,128)(2,1)S(1)}, bf16[2,4,96,384]{3,2,1,0:T(8,128)(2,1)S(1)}, u32[]{:S(2)}, u32[]{:S(2)}) %collective-permute-start.8) | collective-permute-done | bytes 589856 | tf_op jit(solution)/shard_map/ppermute | solution.py:54
  104.5 2.3 collective-permute-start.20
  115.2 4.2 %collective-permute-done.30 = bf16[4,96,384]{2,1,0:T(8,128)(2,1)S(1)} collective-permute-done((bf16[4,96,384]{2,1,0:T(8,128)(2,1)S(1)}, bf16[4,96,384]{2,1,0:T(8,128)(2,1)S(1)}, u32[]{:S(2)}, u32[]{:S(2)}) %collective-permute-start.30) | collective-permute-done | bytes 294944 | tf_op jit(solution)/shard_map/ppermute | solution.py:54
  120.4 8.0 %collective-permute-done.25 = bf16[4,96,768]{2,1,0:T(8,128)(2,1)S(1)} collective-permute-done((bf16[4,96,768]{2,1,0:T(8,128)(2,1)S(1)}, bf16[4,96,768]{2,1,0:T(8,128)(2,1)S(1)}, u32[]{:S(2)}, u32[]{:S(2)}) %collective-permute-start.25) | collective-permute-done | bytes 589856 | tf_op jit(solution)/shard_map/ppermute | solution.py:54
  130.1 1.9 collective-permute-done.21
  136.7 4.5 %fusion.200 = (bf16[1,768,768]{2,1,0:T(8,128)(2,1)}, bf16[1,768,768]{2,1,0:T(8,128)(2,1)S(1)}) fusion(bf16[2,768,768]{2,1,0:T(8,128)(2,1)} %collective-permute-done.10), kind=kLoop, calls=%fused_computation.440 | loop fusion | bytes 4718592 | tf_op jit(solution)/shard_map/slice | solution.py:256
  145.6 2.4 slice.209
  148.0 2.2 slice.205
  152.0 3.4 convolution_convert_fusion
  155.5 2.8 copy.78
  158.3 2.2 reshape.625
  160.5 2.6 fusion.199
  174.7 3.1 fusion.178
  177.8 3.1 fusion.176
  180.9 7.6 %fusion.13 = f32[1024,768]{1,0:T(8,128)} fusion(f32[1024,768]{1,0:T(8,128)} %fusion.178, bf16[768,384]{1,0:T(8,128)(2,1)} %bitcast.608, bf16[768,384]{1,0:T(8,128)(2,1)} %bitcast.85, bf16[768,768]{1,0:T(8,128)(2,1)} %bitcast.64, bf16[512,768]{1,0:T(8,128)(2,1)} %copy-done.94, bf16[512,768]{1,0:T(8,128)(2,1)} %copy-done.37), kind=kOutput, calls=%fused_computation.42 | convolution fusion | flops 2426142720 | bytes 10223616 | tf_op jit(solution)/shard_map/dot_general | solution.py:41
  188.5 8.5 %convolution_add_fusion = f32[1024,768]{1,0:T(8,128)} fusion(f32[1024,768]{1,0:T(8,128)} %fusion.13, f32[1024,768]{1,0:T(8,128)} %fusion.176, bf16[768,384]{1,0:T(8,128)(2,1)} %bitcast.606, bf16[768,384]{1,0:T(8,128)(2,1)} %collective-permute-done.37, bf16[768,768]{1,0:T(8,128)(2,1)} %collective-permute-done.36, bf16[512,768]{1,0:T(8,128)(2,1)} %copy-done.94, ...), kind=kOutput, calls=%fused_computation.26 | convolution fusion | flops 2426929152 | bytes 13369344 | tf_op jit(solution)/shard_map/dot_general | solution.py:41
  197.0 2.7 slice.221
  207.6 2.2 fusion.197
  215.7 1.8 fusion.182
  232.5 1.9 collective-permute-start.58
  244.8 5.8 %fusion.17 = bf16[4,128,1,12,64]{1,4,3,0,2:T(8,128)(2,1)} fusion(bf16[4,12,32,64]{3,1,2,0:T(8,128)(2,1)} %bitcast.610, f32[4,12,32]{2,1,0:T(8,128)} %get-tuple-element.140, f32[4,12,32,128]{3,2,1,0:T(8,128)} %copy-done.32), kind=kOutput, calls=%fused_computation.65 | convolution fusion | flops 26150528 | bytes 1775616 | tf_op jit(solution)/shard_map/bhst,bhse->bhte/dot_general | solution.py:413
  250.6 1.9 multiply_reduce_fusion.2
  255.1 2.6 fusion.19
  257.8 2.1 fusion.124
  261.3 2.2 copy.102
  265.5 3.2 bitcast_add_fusion
  270.1 1.8 fusion.67
  277.3 1.9 fusion.71
  279.4 2.5 maximum_bitcast_fusion.3
  282.0 1.9 collective-permute-start.53
  285.7 1.9 collective-permute-start.54
  301.9 2.1 collective-permute-start.77
  308.1 2.1 collective-permute-start.72
  311.3 3.3 collective-permute-done.72
  314.6 2.8 collective-permute-done.71
  320.8 2.2 collective-permute-start.59
  327.4 7.2 %collective-permute-done.59 = bf16[4,96,768]{2,1,0:T(8,128)(2,1)S(1)} collective-permute-done((bf16[4,96,768]{2,1,0:T(8,128)(2,1)S(1)}, bf16[4,96,768]{2,1,0:T(8,128)(2,1)S(1)}, u32[]{:S(2)}, u32[]{:S(2)}) %collective-permute-start.59) | collective-permute-done | bytes 589856 | tf_op jit(solution)/shard_map/ppermute | solution.py:54
  335.6 2.1 collective-permute-start.62
  337.7 2.3 collective-permute-start.60
  350.9 2.6 collective-permute-start.65
  353.5 2.2 multiply_subtract_fusion.6
  358.0 3.5 collective-permute-done.66
  361.5 2.4 multiply_subtract_fusion.5
  370.5 3.4 collective-permute-done.48
  374.0 5.1 %collective-permute-start.51 = (bf16[96,384]{1,0:T(8,128)(2,1)S(1)}, bf16[96,384]{1,0:T(8,128)(2,1)S(1)}, u32[]{:S(2)}, u32[]{:S(2)}) collective-permute-start(bf16[96,384]{1,0:T(8,128)(2,1)S(1)} %get-tuple-element.120), channel_id=1, source_target_pairs={{0,24},{4,28},{8,16},{12,20},{16,8},{20,12},{24,0},{28,4},{1,25},{... | collective-permute-start | bytes 221192 | tf_op jit(solution)/shard_map/ppermute | solution.py:54
  379.9 3.9 collective-permute-start.46
  387.7 1.9 collective-permute-done.45
  (542 shorter events, 183.1 us)
Async XLA Ops:
  2.5 73.2 %collective-permute-start.22 = (bf16[96,768]{1,0:T(8,128)(2,1)}, bf16[96,768]{1,0:T(8,128)(2,1)}, u32[]{:S(2)}, u32[]{:S(2)}) collective-permute-start(bf16[96,768]{1,0:T(8,128)(2,1)} %get-tuple-element.76), channel_id=1, source_target_pairs={{0,8},{4,12},{8,0},{12,4},{16,24},{20,28},{24,16},{28,20},{1,9},{5... | collective-permute-start | bytes 442376 | tf_op jit(solution)/shard_map/ppermute | solution.py:54
  5.5 103.0 %collective-permute-start.23 = (bf16[96,768]{1,0:T(8,128)(2,1)}, bf16[96,768]{1,0:T(8,128)(2,1)}, u32[]{:S(2)}, u32[]{:S(2)}) collective-permute-start(bf16[96,768]{1,0:T(8,128)(2,1)} %get-tuple-element.76), channel_id=1, source_target_pairs={{0,16},{4,20},{8,24},{12,28},{16,0},{20,4},{24,8},{28,12},{1,17},{... | collective-permute-start | bytes 442376 | tf_op jit(solution)/shard_map/ppermute | solution.py:54
  8.1 101.4 %collective-permute-start.24 = (bf16[96,768]{1,0:T(8,128)(2,1)}, bf16[96,768]{1,0:T(8,128)(2,1)}, u32[]{:S(2)}, u32[]{:S(2)}) collective-permute-start(bf16[96,768]{1,0:T(8,128)(2,1)} %get-tuple-element.76), channel_id=1, source_target_pairs={{0,24},{4,28},{8,16},{12,20},{16,8},{20,12},{24,0},{28,4},{1,25},{... | collective-permute-start | bytes 442376 | tf_op jit(solution)/shard_map/ppermute | solution.py:54
  8.1 15.2 %collective-permute-start.11 = (f32[1,96]{1,0:T(1,128)}, f32[1,96]{1,0:T(1,128)}, u32[]{:S(2)}, u32[]{:S(2)}) collective-permute-start(f32[1,96]{1,0:T(1,128)} %param.34), channel_id=1, source_target_pairs={{0,8},{4,12},{8,0},{12,4},{16,24},{20,28},{24,16},{28,20},{1,9},{5... | collective-permute-start | bytes 1160 | tf_op jit(solution)/shard_map/ppermute | solution.py:54
  9.0 15.0 %collective-permute-start.12 = (f32[1,96]{1,0:T(1,128)}, f32[1,96]{1,0:T(1,128)}, u32[]{:S(2)}, u32[]{:S(2)}) collective-permute-start(f32[1,96]{1,0:T(1,128)} %param.34), channel_id=1, source_target_pairs={{0,16},{4,20},{8,24},{12,28},{16,0},{20,4},{24,8},{28,12},{1,17},{... | collective-permute-start | bytes 1160 | tf_op jit(solution)/shard_map/ppermute | solution.py:54
  24.0 14.7 %collective-permute-start.31 = (bf16[96,384]{1,0:T(8,128)(2,1)S(1)}, bf16[96,384]{1,0:T(8,128)(2,1)S(1)}, u32[]{:S(2)}, u32[]{:S(2)}) collective-permute-start(bf16[96,384]{1,0:T(8,128)(2,1)S(1)} %copy-done.75), channel_id=1, source_target_pairs={{0,8},{4,12},{8,0},{12,4},{16,24},{20,28},{24,16},{28,20},{1,9},{5... | collective-permute-start | bytes 221192 | tf_op jit(solution)/shard_map/ppermute | solution.py:54
  37.5 6.1 %collective-permute-start.32 = (bf16[96,384]{1,0:T(8,128)(2,1)S(1)}, bf16[96,384]{1,0:T(8,128)(2,1)S(1)}, u32[]{:S(2)}, u32[]{:S(2)}) collective-permute-start(bf16[96,384]{1,0:T(8,128)(2,1)S(1)} %copy-done.75), channel_id=1, source_target_pairs={{0,16},{4,20},{8,24},{12,28},{16,0},{20,4},{24,8},{28,12},{1,17},{... | collective-permute-start | bytes 221192 | tf_op jit(solution)/shard_map/ppermute | solution.py:54
  38.7 6.3 %collective-permute-start.33 = (bf16[96,384]{1,0:T(8,128)(2,1)S(1)}, bf16[96,384]{1,0:T(8,128)(2,1)S(1)}, u32[]{:S(2)}, u32[]{:S(2)}) collective-permute-start(bf16[96,384]{1,0:T(8,128)(2,1)S(1)} %copy-done.75), channel_id=1, source_target_pairs={{0,24},{4,28},{8,16},{12,20},{16,8},{20,12},{24,0},{28,4},{1,25},{... | collective-permute-start | bytes 221192 | tf_op jit(solution)/shard_map/ppermute | solution.py:54
  45.0 6.9 %collective-permute-start.5 = (bf16[96,384]{1,0:T(8,128)(2,1)S(1)}, bf16[96,384]{1,0:T(8,128)(2,1)S(1)}, u32[]{:S(2)}, u32[]{:S(2)}) collective-permute-start(bf16[96,384]{1,0:T(8,128)(2,1)S(1)} %get-tuple-element.74), channel_id=1, source_target_pairs={{0,16},{4,20},{8,24},{12,28},{16,0},{20,4},{24,8},{28,12},{1,17},{... | collective-permute-start | bytes 221192 | tf_op jit(solution)/shard_map/ppermute | solution.py:54
  48.4 6.2 %collective-permute-start.6 = (bf16[96,384]{1,0:T(8,128)(2,1)S(1)}, bf16[96,384]{1,0:T(8,128)(2,1)S(1)}, u32[]{:S(2)}, u32[]{:S(2)}) collective-permute-start(bf16[96,384]{1,0:T(8,128)(2,1)S(1)} %get-tuple-element.74), channel_id=1, source_target_pairs={{0,24},{4,28},{8,16},{12,20},{16,8},{20,12},{24,0},{28,4},{1,25},{... | collective-permute-start | bytes 221192 | tf_op jit(solution)/shard_map/ppermute | solution.py:54
  54.6 5.5 %collective-permute-start.1 = (bf16[96,384]{1,0:T(8,128)(2,1)S(1)}, bf16[96,384]{1,0:T(8,128)(2,1)S(1)}, u32[]{:S(2)}, u32[]{:S(2)}) collective-permute-start(bf16[96,384]{1,0:T(8,128)(2,1)S(1)} %slice.200), channel_id=1, source_target_pairs={{0,16},{4,20},{8,24},{12,28},{16,0},{20,4},{24,8},{28,12},{1,17},{... | collective-permute-start | bytes 221192 | tf_op jit(solution)/shard_map/ppermute | solution.py:54
  56.3 6.2 %collective-permute-start.2 = (bf16[96,384]{1,0:T(8,128)(2,1)S(1)}, bf16[96,384]{1,0:T(8,128)(2,1)S(1)}, u32[]{:S(2)}, u32[]{:S(2)}) collective-permute-start(bf16[96,384]{1,0:T(8,128)(2,1)S(1)} %slice.200), channel_id=1, source_target_pairs={{0,24},{4,28},{8,16},{12,20},{16,8},{20,12},{24,0},{28,4},{1,25},{... | collective-permute-start | bytes 221192 | tf_op jit(solution)/shard_map/ppermute | solution.py:54
  60.1 6.0 %collective-permute-start.27 = (bf16[96,384]{1,0:T(8,128)(2,1)S(1)}, bf16[96,384]{1,0:T(8,128)(2,1)S(1)}, u32[]{:S(2)}, u32[]{:S(2)}) collective-permute-start(bf16[96,384]{1,0:T(8,128)(2,1)S(1)} %copy-done.74), channel_id=1, source_target_pairs={{0,8},{4,12},{8,0},{12,4},{16,24},{20,28},{24,16},{28,20},{1,9},{5... | collective-permute-start | bytes 221192 | tf_op jit(solution)/shard_map/ppermute | solution.py:54
  62.5 5.5 %collective-permute-start.28 = (bf16[96,384]{1,0:T(8,128)(2,1)S(1)}, bf16[96,384]{1,0:T(8,128)(2,1)S(1)}, u32[]{:S(2)}, u32[]{:S(2)}) collective-permute-start(bf16[96,384]{1,0:T(8,128)(2,1)S(1)} %copy-done.74), channel_id=1, source_target_pairs={{0,16},{4,20},{8,24},{12,28},{16,0},{20,4},{24,8},{28,12},{1,17},{... | collective-permute-start | bytes 221192 | tf_op jit(solution)/shard_map/ppermute | solution.py:54
  66.2 6.2 %collective-permute-start.29 = (bf16[96,384]{1,0:T(8,128)(2,1)S(1)}, bf16[96,384]{1,0:T(8,128)(2,1)S(1)}, u32[]{:S(2)}, u32[]{:S(2)}) collective-permute-start(bf16[96,384]{1,0:T(8,128)(2,1)S(1)} %copy-done.74), channel_id=1, source_target_pairs={{0,24},{4,28},{8,16},{12,20},{16,8},{20,12},{24,0},{28,4},{1,25},{... | collective-permute-start | bytes 221192 | tf_op jit(solution)/shard_map/ppermute | solution.py:54
  68.0 10.1 %collective-permute-start.34 = (bf16[4,96,384]{2,1,0:T(8,128)(2,1)S(1)}, bf16[4,96,384]{2,1,0:T(8,128)(2,1)S(1)}, u32[]{:S(2)}, u32[]{:S(2)}) collective-permute-start(bf16[4,96,384]{2,1,0:T(8,128)(2,1)S(1)} %bitcast_dynamic-update-slice_fusion.20), channel_id=1, source_target_pairs={{0,2},{1,3},{2,0},{3,1},{4,6},{5,7},{6,4},{7,5},{8,10},{9,11},{10,... | collective-permute-start | bytes 884744 | tf_op jit(solution)/shard_map/ppermute | solution.py:54
  72.4 8.8 %collective-permute-start.7 = (bf16[4,96,384]{2,1,0:T(8,128)(2,1)S(1)}, bf16[4,96,384]{2,1,0:T(8,128)(2,1)S(1)}, u32[]{:S(2)}, u32[]{:S(2)}) collective-permute-start(bf16[4,96,384]{2,1,0:T(8,128)(2,1)S(1)} %bitcast_dynamic-update-slice_fusion.28), channel_id=1, source_target_pairs={{0,2},{1,3},{2,0},{3,1},{4,6},{5,7},{6,4},{7,5},{8,10},{9,11},{10,... | collective-permute-start | bytes 884744 | tf_op jit(solution)/shard_map/ppermute | solution.py:54
  75.7 10.2 %collective-permute-start.3 = (bf16[4,96,384]{2,1,0:T(8,128)(2,1)}, bf16[4,96,384]{2,1,0:T(8,128)(2,1)S(1)}, u32[]{:S(2)}, u32[]{:S(2)}) collective-permute-start(bf16[4,96,384]{2,1,0:T(8,128)(2,1)} %bitcast_dynamic-update-slice_fusion.32), channel_id=1, source_target_pairs={{0,4},{4,0},{8,12},{12,8},{16,20},{20,16},{24,28},{28,24},{1,5},{5... | collective-permute-start | bytes 884744 | tf_op jit(solution)/shard_map/ppermute | solution.py:54
  78.2 18.0 %collective-permute-start.35 = (bf16[2,4,96,384]{3,2,1,0:T(8,128)(2,1)S(1)}, bf16[2,4,96,384]{3,2,1,0:T(8,128)(2,1)S(1)}, u32[]{:S(2)}, u32[]{:S(2)}) collective-permute-start(bf16[2,4,96,384]{3,2,1,0:T(8,128)(2,1)S(1)} %pad_maximum_fusion.12), channel_id=1, source_target_pairs={{0,4},{4,0},{8,12},{12,8},{16,20},{20,16},{24,28},{28,24},{1,5},{5... | collective-permute-start | bytes 1769480 | tf_op jit(solution)/shard_map/ppermute | solution.py:54
  81.3 21.2 %collective-permute-start.8 = (bf16[2,4,96,384]{3,2,1,0:T(8,128)(2,1)S(1)}, bf16[2,4,96,384]{3,2,1,0:T(8,128)(2,1)S(1)}, u32[]{:S(2)}, u32[]{:S(2)}) collective-permute-start(bf16[2,4,96,384]{3,2,1,0:T(8,128)(2,1)S(1)} %pad_maximum_fusion.11), channel_id=1, source_target_pairs={{0,4},{4,0},{8,12},{12,8},{16,20},{20,16},{24,28},{28,24},{1,5},{5... | collective-permute-start | bytes 1769480 | tf_op jit(solution)/shard_map/ppermute | solution.py:54
  85.9 18.6 %collective-permute-start.9 = (bf16[768,384]{1,0:T(8,128)(2,1)S(1)}, bf16[768,384]{1,0:T(8,128)(2,1)S(1)}, u32[]{:S(2)}, u32[]{:S(2)}) collective-permute-start(bf16[768,384]{1,0:T(8,128)(2,1)S(1)} %bitcast.597), channel_id=1, source_target_pairs={{0,2},{1,3},{2,0},{3,1},{4,6},{5,7},{6,4},{7,5},{8,10},{9,11},{10,... | collective-permute-start | bytes 1769480 | tf_op jit(solution)/shard_map/ppermute | solution.py:54
  96.2 15.9 %collective-permute-start.18 = (bf16[96,768]{1,0:T(8,128)(2,1)S(1)}, bf16[96,768]{1,0:T(8,128)(2,1)S(1)}, u32[]{:S(2)}, u32[]{:S(2)}) collective-permute-start(bf16[96,768]{1,0:T(8,128)(2,1)S(1)} %copy-done.70), channel_id=1, source_target_pairs={{0,8},{4,12},{8,0},{12,4},{16,24},{20,28},{24,16},{28,20},{1,9},{5... | collective-permute-start | bytes 442376 | tf_op jit(solution)/shard_map/ppermute | solution.py:54
  102.5 10.2 %collective-permute-start.19 = (bf16[96,768]{1,0:T(8,128)(2,1)S(1)}, bf16[96,768]{1,0:T(8,128)(2,1)S(1)}, u32[]{:S(2)}, u32[]{:S(2)}) collective-permute-start(bf16[96,768]{1,0:T(8,128)(2,1)S(1)} %copy-done.70), channel_id=1, source_target_pairs={{0,16},{4,20},{8,24},{12,28},{16,0},{20,4},{24,8},{28,12},{1,17},{... | collective-permute-start | bytes 442376 | tf_op jit(solution)/shard_map/ppermute | solution.py:54
  104.5 8.3 %collective-permute-start.20 = (bf16[96,768]{1,0:T(8,128)(2,1)S(1)}, bf16[96,768]{1,0:T(8,128)(2,1)S(1)}, u32[]{:S(2)}, u32[]{:S(2)}) collective-permute-start(bf16[96,768]{1,0:T(8,128)(2,1)S(1)} %copy-done.70), channel_id=1, source_target_pairs={{0,24},{4,28},{8,16},{12,20},{16,8},{20,12},{24,0},{28,4},{1,25},{... | collective-permute-start | bytes 442376 | tf_op jit(solution)/shard_map/ppermute | solution.py:54
  108.5 28.2 %collective-permute-start.10 = (bf16[2,768,768]{2,1,0:T(8,128)(2,1)}, bf16[2,768,768]{2,1,0:T(8,128)(2,1)}, u32[]{:S(2)}, u32[]{:S(2)}) collective-permute-start(bf16[2,768,768]{2,1,0:T(8,128)(2,1)} %pad_maximum_fusion), channel_id=1, source_target_pairs={{0,1},{1,0},{2,3},{3,2},{4,5},{5,4},{6,7},{7,6},{8,9},{9,8},{10,11... | collective-permute-start | bytes 7077896 | tf_op jit(solution)/shard_map/ppermute | solution.py:54
  109.5 9.9 %collective-permute-start.30 = (bf16[4,96,384]{2,1,0:T(8,128)(2,1)S(1)}, bf16[4,96,384]{2,1,0:T(8,128)(2,1)S(1)}, u32[]{:S(2)}, u32[]{:S(2)}) collective-permute-start(bf16[4,96,384]{2,1,0:T(8,128)(2,1)S(1)} %bitcast_dynamic-update-slice_fusion.24), channel_id=1, source_target_pairs={{0,4},{4,0},{8,12},{12,8},{16,20},{20,16},{24,28},{28,24},{1,5},{5... | collective-permute-start | bytes 884744 | tf_op jit(solution)/shard_map/ppermute | solution.py:54
  112.2 16.2 %collective-permute-start.25 = (bf16[4,96,768]{2,1,0:T(8,128)(2,1)S(1)}, bf16[4,96,768]{2,1,0:T(8,128)(2,1)S(1)}, u32[]{:S(2)}, u32[]{:S(2)}) collective-permute-start(bf16[4,96,768]{2,1,0:T(8,128)(2,1)S(1)} %bitcast_dynamic-update-slice_fusion.12), channel_id=1, source_target_pairs={{0,2},{1,3},{2,0},{3,1},{4,6},{5,7},{6,4},{7,5},{8,10},{9,11},{10,... | collective-permute-start | bytes 1769480 | tf_op jit(solution)/shard_map/ppermute | solution.py:54
  112.8 19.2 %collective-permute-start.21 = (bf16[4,96,768]{2,1,0:T(8,128)(2,1)S(1)}, bf16[4,96,768]{2,1,0:T(8,128)(2,1)S(1)}, u32[]{:S(2)}, u32[]{:S(2)}) collective-permute-start(bf16[4,96,768]{2,1,0:T(8,128)(2,1)S(1)} %bitcast_dynamic-update-slice_fusion.16), channel_id=1, source_target_pairs={{0,4},{4,0},{8,12},{12,8},{16,20},{20,16},{24,28},{28,24},{1,5},{5... | collective-permute-start | bytes 1769480 | tf_op jit(solution)/shard_map/ppermute | solution.py:54
  120.1 68.3 %collective-permute-start.37 = (bf16[768,384]{1,0:T(8,128)(2,1)}, bf16[768,384]{1,0:T(8,128)(2,1)}, u32[]{:S(2)}, u32[]{:S(2)}) collective-permute-start(bf16[768,384]{1,0:T(8,128)(2,1)} %bitcast.85), channel_id=1, source_target_pairs={{0,2},{1,3},{2,0},{3,1},{4,6},{5,7},{6,4},{7,5},{8,10},{9,11},{10,... | collective-permute-start | bytes 1769480 | tf_op jit(solution)/shard_map/ppermute | solution.py:54
  129.6 41.3 %collective-permute-start.26 = (bf16[2,4,96,768]{3,2,1,0:T(8,128)(2,1)}, bf16[2,4,96,768]{3,2,1,0:T(8,128)(2,1)}, u32[]{:S(2)}, u32[]{:S(2)}) collective-permute-start(bf16[2,4,96,768]{3,2,1,0:T(8,128)(2,1)} %pad_maximum_fusion.4), channel_id=1, source_target_pairs={{0,4},{4,0},{8,12},{12,8},{16,20},{20,16},{24,28},{28,24},{1,5},{5... | collective-permute-start | bytes 3538952 | tf_op jit(solution)/shard_map/ppermute | solution.py:54
  132.9 55.5 %collective-permute-start.36 = (bf16[768,768]{1,0:T(8,128)(2,1)}, bf16[768,768]{1,0:T(8,128)(2,1)}, u32[]{:S(2)}, u32[]{:S(2)}) collective-permute-start(bf16[768,768]{1,0:T(8,128)(2,1)} %bitcast.64), channel_id=1, source_target_pairs={{0,2},{1,3},{2,0},{3,1},{4,6},{5,7},{6,4},{7,5},{8,10},{9,11},{10,... | collective-permute-start | bytes 3538952 | tf_op jit(solution)/shard_map/ppermute | solution.py:54
  199.7 7.5 %collective-permute-start.38 = (f32[512,768]{1,0:T(8,128)}, f32[512,768]{1,0:T(8,128)}, u32[]{:S(2)}, u32[]{:S(2)}) collective-permute-start(f32[512,768]{1,0:T(8,128)} %slice.221), channel_id=1, source_target_pairs={{0,1},{1,0},{2,3},{3,2},{4,5},{5,4},{6,7},{7,6},{8,9},{9,8},{10,11... | collective-permute-start | bytes 4718600 | tf_op jit(solution)/shard_map/ppermute | solution.py:54
  231.3 10.8 %collective-permute-start.40 = (f32[128,768]{1,0:T(8,128)S(1)}, f32[128,768]{1,0:T(8,128)S(1)}, u32[]{:S(2)}, u32[]{:S(2)}) collective-permute-start(f32[128,768]{1,0:T(8,128)S(1)} %slice.227), channel_id=1, source_target_pairs={{0,1},{1,0},{2,3},{3,2},{4,5},{5,4},{6,7},{7,6},{8,9},{9,8},{10,11... | collective-permute-start | bytes 1179656 | tf_op jit(solution)/shard_map/ppermute | solution.py:54
  232.5 86.5 %collective-permute-start.58 = (bf16[4,2,96,768]{3,2,0,1:T(8,128)(2,1)}, bf16[4,2,96,768]{3,2,0,1:T(8,128)(2,1)}, u32[]{:S(2)}, u32[]{:S(2)}) collective-permute-start(bf16[4,2,96,768]{3,2,0,1:T(8,128)(2,1)} %copy.110), channel_id=1, source_target_pairs={{0,2},{1,3},{2,0},{3,1},{4,6},{5,7},{6,4},{7,5},{8,10},{9,11},{10,... | collective-permute-start | bytes 3538952 | tf_op jit(solution)/shard_map/ppermute | solution.py:54
  235.5 87.5 %collective-permute-start.63 = (bf16[2,4,96,768]{3,2,1,0:T(8,128)(2,1)}, bf16[2,4,96,768]{3,2,1,0:T(8,128)(2,1)}, u32[]{:S(2)}, u32[]{:S(2)}) collective-permute-start(bf16[2,4,96,768]{3,2,1,0:T(8,128)(2,1)} %fusion.27), channel_id=1, source_target_pairs={{0,4},{4,0},{8,12},{12,8},{16,20},{20,16},{24,28},{28,24},{1,5},{5... | collective-permute-start | bytes 3538952 | tf_op jit(solution)/shard_map/ppermute | solution.py:54
  239.0 53.6 %collective-permute-start.73 = (bf16[2,4,96,384]{3,2,1,0:T(8,128)(2,1)}, bf16[2,4,96,384]{3,2,1,0:T(8,128)(2,1)}, u32[]{:S(2)}, u32[]{:S(2)}) collective-permute-start(bf16[2,4,96,384]{3,2,1,0:T(8,128)(2,1)} %fusion.54), channel_id=1, source_target_pairs={{0,4},{4,0},{8,12},{12,8},{16,20},{20,16},{24,28},{28,24},{1,5},{5... | collective-permute-start | bytes 1769480 | tf_op jit(solution)/shard_map/ppermute | solution.py:54
  240.4 49.1 %collective-permute-start.68 = (bf16[4,2,96,384]{3,2,0,1:T(8,128)(2,1)}, bf16[4,2,96,384]{3,2,0,1:T(8,128)(2,1)}, u32[]{:S(2)}, u32[]{:S(2)}) collective-permute-start(bf16[4,2,96,384]{3,2,0,1:T(8,128)(2,1)} %copy.114), channel_id=1, source_target_pairs={{0,2},{1,3},{2,0},{3,1},{4,6},{5,7},{6,4},{7,5},{8,10},{9,11},{10,... | collective-permute-start | bytes 1769480 | tf_op jit(solution)/shard_map/ppermute | solution.py:54
  290.8 8.0 %collective-permute-start.69 = (bf16[4,96,384]{2,1,0:T(8,128)(2,1)S(1)}, bf16[4,96,384]{2,1,0:T(8,128)(2,1)S(1)}, u32[]{:S(2)}, u32[]{:S(2)}) collective-permute-start(bf16[4,96,384]{2,1,0:T(8,128)(2,1)S(1)} %dynamic-slice_bitcast_fusion.1), channel_id=1, source_target_pairs={{0,4},{4,0},{8,12},{12,8},{16,20},{20,16},{24,28},{28,24},{1,5},{5... | collective-permute-start | bytes 884744 | tf_op jit(solution)/shard_map/ppermute | solution.py:54
  294.1 6.8 %collective-permute-start.74 = (bf16[4,96,384]{2,1,0:T(8,128)(2,1)S(1)}, bf16[4,96,384]{2,1,0:T(8,128)(2,1)S(1)}, u32[]{:S(2)}, u32[]{:S(2)}) collective-permute-start(bf16[4,96,384]{2,1,0:T(8,128)(2,1)S(1)} %slice_bitcast_fusion.6), channel_id=1, source_target_pairs={{0,2},{1,3},{2,0},{3,1},{4,6},{5,7},{6,4},{7,5},{8,10},{9,11},{10,... | collective-permute-start | bytes 884744 | tf_op jit(solution)/shard_map/ppermute | solution.py:54
  295.7 6.2 %collective-permute-start.57 = (f32[1,96]{1,0:T(1,128)S(1)}, f32[1,96]{1,0:T(1,128)S(1)}, u32[]{:S(2)}, u32[]{:S(2)}) collective-permute-start(f32[1,96]{1,0:T(1,128)S(1)} %get-tuple-element.130), channel_id=1, source_target_pairs={{0,24},{4,28},{8,16},{12,20},{16,8},{20,12},{24,0},{28,4},{1,25},{... | collective-permute-start | bytes 1160 | tf_op jit(solution)/shard_map/ppermute | solution.py:54
  301.9 6.2 %collective-permute-start.77 = (bf16[96,384]{1,0:T(8,128)(2,1)S(1)}, bf16[96,384]{1,0:T(8,128)(2,1)S(1)}, u32[]{:S(2)}, u32[]{:S(2)}) collective-permute-start(bf16[96,384]{1,0:T(8,128)(2,1)S(1)} %get-tuple-element.114), channel_id=1, source_target_pairs={{0,24},{4,28},{8,16},{12,20},{16,8},{20,12},{24,0},{28,4},{1,25},{... | collective-permute-start | bytes 221192 | tf_op jit(solution)/shard_map/ppermute | solution.py:54
  304.0 6.8 %collective-permute-start.76 = (bf16[96,384]{1,0:T(8,128)(2,1)S(1)}, bf16[96,384]{1,0:T(8,128)(2,1)S(1)}, u32[]{:S(2)}, u32[]{:S(2)}) collective-permute-start(bf16[96,384]{1,0:T(8,128)(2,1)S(1)} %get-tuple-element.115), channel_id=1, source_target_pairs={{0,16},{4,20},{8,24},{12,28},{16,0},{20,4},{24,8},{28,12},{1,17},{... | collective-permute-start | bytes 221192 | tf_op jit(solution)/shard_map/ppermute | solution.py:54
  304.7 6.0 %collective-permute-start.75 = (bf16[96,384]{1,0:T(8,128)(2,1)S(1)}, bf16[96,384]{1,0:T(8,128)(2,1)S(1)}, u32[]{:S(2)}, u32[]{:S(2)}) collective-permute-start(bf16[96,384]{1,0:T(8,128)(2,1)S(1)} %get-tuple-element.113), channel_id=1, source_target_pairs={{0,8},{4,12},{8,0},{12,4},{16,24},{20,28},{24,16},{28,20},{1,9},{5... | collective-permute-start | bytes 221192 | tf_op jit(solution)/shard_map/ppermute | solution.py:54
  308.1 6.5 %collective-permute-start.72 = (bf16[96,384]{1,0:T(8,128)(2,1)S(1)}, bf16[96,384]{1,0:T(8,128)(2,1)S(1)}, u32[]{:S(2)}, u32[]{:S(2)}) collective-permute-start(bf16[96,384]{1,0:T(8,128)(2,1)S(1)} %get-tuple-element.111), channel_id=1, source_target_pairs={{0,24},{4,28},{8,16},{12,20},{16,8},{20,12},{24,0},{28,4},{1,25},{... | collective-permute-start | bytes 221192 | tf_op jit(solution)/shard_map/ppermute | solution.py:54
  310.8 29.4 %collective-permute-start.41 = (bf16[2,768,768]{1,2,0:T(8,128)(2,1)S(1)}, bf16[2,768,768]{1,2,0:T(8,128)(2,1)S(1)}, u32[]{:S(2)}, u32[]{:S(2)}) collective-permute-start(bf16[2,768,768]{1,2,0:T(8,128)(2,1)S(1)} %pad_maximum_fusion.2), channel_id=1, source_target_pairs={{0,1},{1,0},{2,3},{3,2},{4,5},{5,4},{6,7},{7,6},{8,9},{9,8},{10,11... | collective-permute-start | bytes 7077896 | tf_op jit(solution)/shard_map/ppermute | solution.py:54
  310.8 6.6 %collective-permute-start.71 = (bf16[96,384]{1,0:T(8,128)(2,1)S(1)}, bf16[96,384]{1,0:T(8,128)(2,1)S(1)}, u32[]{:S(2)}, u32[]{:S(2)}) collective-permute-start(bf16[96,384]{1,0:T(8,128)(2,1)S(1)} %get-tuple-element.112), channel_id=1, source_target_pairs={{0,16},{4,20},{8,24},{12,28},{16,0},{20,4},{24,8},{28,12},{1,17},{... | collective-permute-start | bytes 221192 | tf_op jit(solution)/shard_map/ppermute | solution.py:54
  320.8 13.9 %collective-permute-start.59 = (bf16[4,96,768]{2,1,0:T(8,128)(2,1)S(1)}, bf16[4,96,768]{2,1,0:T(8,128)(2,1)S(1)}, u32[]{:S(2)}, u32[]{:S(2)}) collective-permute-start(bf16[4,96,768]{2,1,0:T(8,128)(2,1)S(1)} %dynamic-slice_bitcast_fusion), channel_id=1, source_target_pairs={{0,4},{4,0},{8,12},{12,8},{16,20},{20,16},{24,28},{28,24},{1,5},{5... | collective-permute-start | bytes 1769480 | tf_op jit(solution)/shard_map/ppermute | solution.py:54
  324.7 15.4 %collective-permute-start.64 = (bf16[4,96,768]{2,1,0:T(8,128)(2,1)S(1)}, bf16[4,96,768]{2,1,0:T(8,128)(2,1)S(1)}, u32[]{:S(2)}, u32[]{:S(2)}) collective-permute-start(bf16[4,96,768]{2,1,0:T(8,128)(2,1)S(1)} %slice_bitcast_fusion.2), channel_id=1, source_target_pairs={{0,2},{1,3},{2,0},{3,1},{4,6},{5,7},{6,4},{7,5},{8,10},{9,11},{10,... | collective-permute-start | bytes 1769480 | tf_op jit(solution)/shard_map/ppermute | solution.py:54
  335.6 15.3 %collective-permute-start.62 = (bf16[96,768]{1,0:T(8,128)(2,1)}, bf16[96,768]{1,0:T(8,128)(2,1)}, u32[]{:S(2)}, u32[]{:S(2)}) collective-permute-start(bf16[96,768]{1,0:T(8,128)(2,1)} %get-tuple-element.102), channel_id=1, source_target_pairs={{0,24},{4,28},{8,16},{12,20},{16,8},{20,12},{24,0},{28,4},{1,25},{... | collective-permute-start | bytes 442376 | tf_op jit(solution)/shard_map/ppermute | solution.py:54
  337.7 13.2 %collective-permute-start.61 = (bf16[96,768]{1,0:T(8,128)(2,1)}, bf16[96,768]{1,0:T(8,128)(2,1)}, u32[]{:S(2)}, u32[]{:S(2)}) collective-permute-start(bf16[96,768]{1,0:T(8,128)(2,1)} %get-tuple-element.103), channel_id=1, source_target_pairs={{0,16},{4,20},{8,24},{12,28},{16,0},{20,4},{24,8},{28,12},{1,17},{... | collective-permute-start | bytes 442376 | tf_op jit(solution)/shard_map/ppermute | solution.py:54
  337.7 15.8 %collective-permute-start.60 = (bf16[96,768]{1,0:T(8,128)(2,1)}, bf16[96,768]{1,0:T(8,128)(2,1)}, u32[]{:S(2)}, u32[]{:S(2)}) collective-permute-start(bf16[96,768]{1,0:T(8,128)(2,1)} %get-tuple-element.101), channel_id=1, source_target_pairs={{0,8},{4,12},{8,0},{12,4},{16,24},{20,28},{24,16},{28,20},{1,9},{5... | collective-permute-start | bytes 442376 | tf_op jit(solution)/shard_map/ppermute | solution.py:54
  346.6 17.7 %collective-permute-start.47 = (bf16[2,4,96,384]{3,2,1,0:T(8,128)(2,1)}, bf16[2,4,96,384]{3,2,1,0:T(8,128)(2,1)}, u32[]{:S(2)}, u32[]{:S(2)}) collective-permute-start(bf16[2,4,96,384]{3,2,1,0:T(8,128)(2,1)} %fusion.58), channel_id=1, source_target_pairs={{0,4},{4,0},{8,12},{12,8},{16,20},{20,16},{24,28},{28,24},{1,5},{5... | collective-permute-start | bytes 1769480 | tf_op jit(solution)/shard_map/ppermute | solution.py:54
  349.1 8.9 %collective-permute-start.67 = (bf16[96,768]{1,0:T(8,128)(2,1)}, bf16[96,768]{1,0:T(8,128)(2,1)}, u32[]{:S(2)}, u32[]{:S(2)}) collective-permute-start(bf16[96,768]{1,0:T(8,128)(2,1)} %get-tuple-element.99), channel_id=1, source_target_pairs={{0,24},{4,28},{8,16},{12,20},{16,8},{20,12},{24,0},{28,4},{1,25},{... | collective-permute-start | bytes 442376 | tf_op jit(solution)/shard_map/ppermute | solution.py:54
  350.9 10.6 %collective-permute-start.66 = (bf16[96,768]{1,0:T(8,128)(2,1)}, bf16[96,768]{1,0:T(8,128)(2,1)}, u32[]{:S(2)}, u32[]{:S(2)}) collective-permute-start(bf16[96,768]{1,0:T(8,128)(2,1)} %get-tuple-element.100), channel_id=1, source_target_pairs={{0,16},{4,20},{8,24},{12,28},{16,0},{20,4},{24,8},{28,12},{1,17},{... | collective-permute-start | bytes 442376 | tf_op jit(solution)/shard_map/ppermute | solution.py:54
  350.9 10.6 %collective-permute-start.65 = (bf16[96,768]{1,0:T(8,128)(2,1)}, bf16[96,768]{1,0:T(8,128)(2,1)}, u32[]{:S(2)}, u32[]{:S(2)}) collective-permute-start(bf16[96,768]{1,0:T(8,128)(2,1)} %get-tuple-element.98), channel_id=1, source_target_pairs={{0,8},{4,12},{8,0},{12,4},{16,24},{20,28},{24,16},{28,20},{1,9},{5... | collective-permute-start | bytes 442376 | tf_op jit(solution)/shard_map/ppermute | solution.py:54
  356.8 11.1 %collective-permute-start.42 = (bf16[4,2,96,384]{3,2,1,0:T(8,128)(2,1)}, bf16[4,2,96,384]{3,2,1,0:T(8,128)(2,1)}, u32[]{:S(2)}, u32[]{:S(2)}) collective-permute-start(bf16[4,2,96,384]{3,2,1,0:T(8,128)(2,1)} %bitcast.605), channel_id=1, source_target_pairs={{0,2},{1,3},{2,0},{3,1},{4,6},{5,7},{6,4},{7,5},{8,10},{9,11},{10,... | collective-permute-start | bytes 1769480 | tf_op jit(solution)/shard_map/ppermute | solution.py:54
  365.6 8.3 %collective-permute-start.48 = (bf16[4,96,384]{2,1,0:T(8,128)(2,1)S(1)}, bf16[4,96,384]{2,1,0:T(8,128)(2,1)S(1)}, u32[]{:S(2)}, u32[]{:S(2)}) collective-permute-start(bf16[4,96,384]{2,1,0:T(8,128)(2,1)S(1)} %slice_bitcast_fusion.8), channel_id=1, source_target_pairs={{0,2},{1,3},{2,0},{3,1},{4,6},{5,7},{6,4},{7,5},{8,10},{9,11},{10,... | collective-permute-start | bytes 884744 | tf_op jit(solution)/shard_map/ppermute | solution.py:54
  369.1 10.6 %collective-permute-start.43 = (bf16[4,96,384]{2,1,0:T(8,128)(2,1)S(1)}, bf16[4,96,384]{2,1,0:T(8,128)(2,1)S(1)}, u32[]{:S(2)}, u32[]{:S(2)}) collective-permute-start(bf16[4,96,384]{2,1,0:T(8,128)(2,1)S(1)} %dynamic-slice_bitcast_fusion.2), channel_id=1, source_target_pairs={{0,4},{4,0},{8,12},{12,8},{16,20},{20,16},{24,28},{28,24},{1,5},{5... | collective-permute-start | bytes 884744 | tf_op jit(solution)/shard_map/ppermute | solution.py:54
  374.0 9.8 %collective-permute-start.51 = (bf16[96,384]{1,0:T(8,128)(2,1)S(1)}, bf16[96,384]{1,0:T(8,128)(2,1)S(1)}, u32[]{:S(2)}, u32[]{:S(2)}) collective-permute-start(bf16[96,384]{1,0:T(8,128)(2,1)S(1)} %get-tuple-element.120), channel_id=1, source_target_pairs={{0,24},{4,28},{8,16},{12,20},{16,8},{20,12},{24,0},{28,4},{1,25},{... | collective-permute-start | bytes 221192 | tf_op jit(solution)/shard_map/ppermute | solution.py:54
  379.1 7.7 %collective-permute-start.50 = (bf16[96,384]{1,0:T(8,128)(2,1)S(1)}, bf16[96,384]{1,0:T(8,128)(2,1)S(1)}, u32[]{:S(2)}, u32[]{:S(2)}) collective-permute-start(bf16[96,384]{1,0:T(8,128)(2,1)S(1)} %get-tuple-element.121), channel_id=1, source_target_pairs={{0,16},{4,20},{8,24},{12,28},{16,0},{20,4},{24,8},{28,12},{1,17},{... | collective-permute-start | bytes 221192 | tf_op jit(solution)/shard_map/ppermute | solution.py:54
  379.1 7.7 %collective-permute-start.49 = (bf16[96,384]{1,0:T(8,128)(2,1)S(1)}, bf16[96,384]{1,0:T(8,128)(2,1)S(1)}, u32[]{:S(2)}, u32[]{:S(2)}) collective-permute-start(bf16[96,384]{1,0:T(8,128)(2,1)S(1)} %get-tuple-element.119), channel_id=1, source_target_pairs={{0,8},{4,12},{8,0},{12,4},{16,24},{20,28},{24,16},{28,20},{1,9},{5... | collective-permute-start | bytes 221192 | tf_op jit(solution)/shard_map/ppermute | solution.py:54
  379.9 7.8 %collective-permute-start.46 = (bf16[96,384]{1,0:T(8,128)(2,1)S(1)}, bf16[96,384]{1,0:T(8,128)(2,1)S(1)}, u32[]{:S(2)}, u32[]{:S(2)}) collective-permute-start(bf16[96,384]{1,0:T(8,128)(2,1)S(1)} %get-tuple-element.117), channel_id=1, source_target_pairs={{0,24},{4,28},{8,16},{12,20},{16,8},{20,12},{24,0},{28,4},{1,25},{... | collective-permute-start | bytes 221192 | tf_op jit(solution)/shard_map/ppermute | solution.py:54
  383.8 5.9 %collective-permute-start.45 = (bf16[96,384]{1,0:T(8,128)(2,1)S(1)}, bf16[96,384]{1,0:T(8,128)(2,1)S(1)}, u32[]{:S(2)}, u32[]{:S(2)}) collective-permute-start(bf16[96,384]{1,0:T(8,128)(2,1)S(1)} %get-tuple-element.118), channel_id=1, source_target_pairs={{0,16},{4,20},{8,24},{12,28},{16,0},{20,4},{24,8},{28,12},{1,17},{... | collective-permute-start | bytes 221192 | tf_op jit(solution)/shard_map/ppermute | solution.py:54
  383.8 5.9 %collective-permute-start.44 = (bf16[96,384]{1,0:T(8,128)(2,1)S(1)}, bf16[96,384]{1,0:T(8,128)(2,1)S(1)}, u32[]{:S(2)}, u32[]{:S(2)}) collective-permute-start(bf16[96,384]{1,0:T(8,128)(2,1)S(1)} %get-tuple-element.116), channel_id=1, source_target_pairs={{0,8},{4,12},{8,0},{12,4},{16,24},{20,28},{24,16},{28,20},{1,9},{5... | collective-permute-start | bytes 221192 | tf_op jit(solution)/shard_map/ppermute | solution.py:54
  (109 other events, 753.2 us)
